TPU v7x, 128 devices: a whole 4x4x4 slice. The times are simulated.
128 devices in a mesh: grp: 8 (over z_lo, x), tp: 16 (over y, z_hi, core).
Axes of the slice: x: 4, y: 4, z: 4 (z_hi: 2, z_lo: 2; z = z_hi * 2 + z_lo), core: 2. Of those that a mesh axis runs over, the one named last changes fastest.
Arguments:
- old_weight: bfloat16 [8192, 8192], P(None, 'tp'), may hold values from -0.0625 to 0.0625
- delta_codes: int32 [8192, 8192], P(('grp', 'tp')), may hold values from -120 to 120
- delta_exps: int32 [8192, 64], P(('grp', 'tp')), may hold values from -14 to -12
- state_in: float32 [192, 128, 64, 128], P('grp', 'tp'), may hold values from -6 to 6
- x_in: bfloat16 [4, 192, 8192], P(None, 'grp', 'tp'), may hold values from -6 to 6
- z_in: bfloat16 [4, 192, 8192], P(None, 'grp', 'tp'), may hold values from -6 to 6
- b_in: bfloat16 [4, 192, 512], P(None, 'grp'), may hold values from -6 to 6
- c_in: bfloat16 [4, 192, 512], P(None, 'grp'), may hold values from -0.5 to 0.5
- dt_in: bfloat16 [4, 192, 128], P(None, 'grp', 'tp'), may hold values from -4 to 4
- dt_bias: float32 [128], P('tp'), may hold values from -3 to 0.5
- a_rate: float32 [128], P('tp'), may hold values from 0.05 to 4
- skip_gain: float32 [128], P('tp'), may hold values from 0.5 to 1.5
- norm_gain: float32 [8192], P('tp'), may hold values from 0.5 to 1.5
Outputs:
- mixed: bfloat16 [4, 192, 8192], P(None, 'grp', 'tp')
- final_state: float32 [192, 128, 64, 128], P('grp', 'tp')
All inputs are finite; a program needn't handle non-finite values.
Results may differ from a plain program's by a relative error of at most 0.0058.
Values may be sent and summed in bfloat16 or wider, within the bound.
A program may use at most 128 MiB of HBM per device.

v0:
```python
import jax
import jax.numpy as jnp
from jax import lax
from jax.sharding import PartitionSpec as P

HEADS = 128
HEAD_P = 64


def local(
    old_weight,
    delta_codes,
    delta_exps,
    state_in,
    x_in,
    z_in,
    b_in,
    c_in,
    dt_in,
    dt_bias,
    a_rate,
    skip_gain,
    norm_gain,
):
    tp_count = lax.axis_size("tp")
    grp_count = lax.axis_size("grp")
    shard_rows, inner_width = delta_codes.shape
    block_count = delta_exps.shape[1]
    block_scale = jnp.exp2(delta_exps.astype(jnp.float32))
    delta_part = (
        (
            delta_codes.astype(jnp.float32).reshape(
                shard_rows, block_count, inner_width // block_count
            )
            * block_scale[:, :, None]
        )
        .reshape(shard_rows, inner_width)
        .astype(jnp.bfloat16)
    )
    grouped_rows = lax.all_gather(delta_part, "grp", axis=0, tiled=True)
    engine_block = lax.all_to_all(grouped_rows, "tp", split_axis=1, concat_axis=0, tiled=True)
    local_cols = engine_block.shape[1]
    full_delta = (
        engine_block.reshape(tp_count, grp_count, shard_rows, local_cols)
        .swapaxes(0, 1)
        .reshape(tp_count * grp_count * shard_rows, local_cols)
    )
    new_weight = (old_weight.astype(jnp.float32) + full_delta.astype(jnp.float32)).astype(
        jnp.bfloat16
    )
    step_count, row_count, local_width = x_in.shape
    heads_local = state_in.shape[1]
    head_width = state_in.shape[2]
    state_width = state_in.shape[3]
    groups = b_in.shape[2] // state_width
    group_index = lax.axis_index("tp") * heads_local // (HEADS // groups)
    b_local = lax.dynamic_index_in_dim(
        b_in.reshape(step_count, row_count, groups, state_width), group_index, 2, keepdims=False
    ).astype(jnp.float32)
    c_local = lax.dynamic_index_in_dim(
        c_in.reshape(step_count, row_count, groups, state_width), group_index, 2, keepdims=False
    ).astype(jnp.float32)
    group_width = HEADS * HEAD_P // groups
    selector = (jnp.arange(groups)[None, :] == group_index).astype(jnp.float32)
    carried = state_in
    outputs = []
    for step_index in range(step_count):
        local_carried = carried
        step_size = jax.nn.softplus(dt_in[step_index].astype(jnp.float32) + dt_bias)
        decay_factor = jnp.exp(-step_size * a_rate)
        x_heads = x_in[step_index].astype(jnp.float32).reshape(row_count, heads_local, head_width)
        local_carried = (
            decay_factor[:, :, None, None] * local_carried
            + (step_size[:, :, None] * x_heads)[:, :, :, None]
            * b_local[step_index][:, None, None, :]
        )
        read_out = (
            jnp.einsum(
                "rhpn,rn->rhp", local_carried, c_local[step_index], precision=lax.Precision.HIGHEST
            )
            + skip_gain[None, :, None] * x_heads
        )
        gated_value = read_out.reshape(row_count, local_width) * jax.nn.silu(
            z_in[step_index].astype(jnp.float32)
        )
        carried, gated_value = (local_carried, gated_value)
        totals = lax.psum(jnp.sum(gated_value * gated_value, axis=1)[:, None] * selector, "tp")
        own_total = jnp.sum(totals * selector, axis=1, keepdims=True)
        normed = (gated_value * lax.rsqrt(own_total / group_width + 1e-05) * norm_gain).astype(
            jnp.bfloat16
        )
        partial_value = lax.dot_general(
            normed, new_weight, (((1,), (1,)), ((), ())), preferred_element_type=jnp.float32
        )
        outputs.append(
            lax.psum_scatter(partial_value, "tp", scatter_dimension=1, tiled=True).astype(
                jnp.bfloat16
            )
        )
    mixed = jnp.stack(outputs)
    return (mixed, carried)


def solution(mesh):
    return jax.shard_map(
        local,
        mesh=mesh,
        in_specs=(
            P(None, "tp"),
            P(("grp", "tp"), None),
            P(("grp", "tp"), None),
            P("grp", "tp", None, None),
            P(None, "grp", "tp"),
            P(None, "grp", "tp"),
            P(None, "grp", None),
            P(None, "grp", None),
            P(None, "grp", "tp"),
            P("tp"),
            P("tp"),
            P("tp"),
            P("tp"),
        ),
        out_specs=(P(None, "grp", "tp"), P("grp", "tp", None, None)),
        check_vma=False,
    )
```

profile of v0, /device:TPU:1, one launch (start us, length us, event | category | flops | bytes accessed | tf_op | source)
XLA Modules:
  0.0 601.1 jit_solution(13572580179550752879)
XLA Ops:
  7.2 0.0 all-gather.2.cloned.1.call-start
  7.2 0.8 multiply_exponential_fusion
  8.0 0.6 mul.441
  8.6 3.9 fusion.9
  12.4 0.0 all-gather.2.cloned.1.call-update
  12.5 95.3 %all-gather.2.cloned.1.call-done = bf16[512,8192]{1,0:T(8,128)(2,1)} async-done(((bf16[64,8192]{1,0:T(8,128)(2,1)}), bf16[512,8192]{1,0:T(8,128)(2,1)}) %all-gather.2.cloned.1.call-update) | async-done | bytes 8388624 | tf_op jit(solution)/shard_map/all_gather | solution.py:40
  107.8 12.0 %copy.83 = bf16[512,8192]{0,1:T(8,128)(2,1)} copy(bf16[512,8192]{1,0:T(8,128)(2,1)} %all-gather.2.cloned.1.call-done) | data formatting | bytes 16777216 | tf_op jit(solution)/shard_map/all_gather | solution.py:40
  119.8 12.3 %copy.84 = bf16[512,16,512]{2,0,1:T(8,128)(2,1)} copy(bf16[512,16,512]{0,2,1:T(8,128)(2,1)} %bitcast.157) | data formatting | bytes 16777216 | tf_op jit(solution)/shard_map/all_to_all | solution.py:41
  132.1 7.4 %all-to-all-start = ((bf16[512,16,512]{2,0,1:T(8,128)(2,1)}), bf16[512,16,512]{2,0,1:T(8,128)(2,1)}, u32[]{:S(2)}, u32[]{:S(2)}) async-start(bf16[512,16,512]{2,0,1:T(8,128)(2,1)} %copy.84), calls=%async_computation | async-start | bytes 16777216 | tf_op jit(solution)/shard_map/all_to_all | solution.py:41
  139.6 0.2 reduce-scatter.11.cloned.1.call-start
  139.8 0.1 reshape.424
  140.0 0.1 reshape.422
  140.1 0.1 multiply_exponential_fusion.3
  140.2 0.1 copy.89
  140.3 0.1 reshape.418
  140.4 0.1 copy.87
  140.4 0.1 copy.88
  140.5 0.1 copy.86
  140.6 0.1 reshape.426
  140.7 0.1 copy.91
  140.7 0.1 reshape.413
  140.8 0.1 copy.81
  140.9 0.1 copy.80
  141.0 0.1 reshape.420
  141.1 0.1 reshape.428
  141.2 0.1 copy.90
  141.2 0.1 reshape.415
  141.3 0.1 constant_dynamic-slice_fusion
  141.4 0.1 broadcast_multiply_fusion.1
  141.5 0.1 broadcast_multiply_fusion
  141.7 9.9 %multiply_add_fusion = f32[24,8,64,128]{3,2,1,0:T(8,128)S(1)} fusion(f32[24,128]{1,0:T(8,128)S(1)} %get-tuple-element.27, f32[24,8,64]{2,1,0:T(8,128)S(1)} %get-tuple-element.50, f32[24,8]{1,0:T(8,128)S(1)} %copy.90, f32[24,128]{1,0:T(8,128)S(1)} %get-tuple-element.28, f32[24,8,64]{2,1,0:T(8,128)S(1)} %get-tuple-element.48, f32[24,8]{1,0:T(8,128)S(1)} %copy.88, ...), kind=kLoop, calls=%fused_computation.2 | loop fusion | flops 18874368 | bytes 12831744 | tf_op jit(solution)/shard_map/add | solution.py:73
  151.6 7.4 %fusion.59 = f32[24,1,8,64]{3,1,2,0:T(1,128)S(1)} fusion(f32[24,8,64,128]{3,2,1,0:T(8,128)S(1)} %multiply_add_fusion, bf16[4,24,4,128]{3,2,1,0:T(4,128)(2,1)S(1)} %reshape.407, s32[]{:T(128)S(6)} %add.242, s32[]{:T(128)S(6)} %select_n.57), kind=kOutput, calls=%fused_computation.97 | convolution fusion | flops 18874368 | bytes 6352904 | tf_op jit(solution)/shard_map/rhpn,rn->rhp/dot_general | solution.py:78
  159.0 8.2 %fusion.1 = f32[24,1,8,64]{3,1,2,0:T(1,128)S(1)} fusion(f32[24,8,64,128]{3,2,1,0:T(8,128)S(1)} %bitcast.159, f32[24,128]{1,0:T(8,128)S(1)} %get-tuple-element.26, f32[24,8,64]{2,1,0:T(8,128)S(1)} %get-tuple-element.51, f32[24,8]{1,0:T(8,128)S(1)} %copy.80, bf16[4,24,4,128]{3,2,1,0:T(4,128)(2,1)S(1)} %reshape.407, s32[]{:T(128)S(6)} %select_n.57), kind=kOutput, calls=%fused_computation.6 | convolution fusion | flops 23592960 | bytes 6475780 | tf_op jit(solution)/shard_map/rhpn,rn->rhp/dot_general | solution.py:78
  167.2 10.9 %fusion.10 = f32[24,1,8,64]{3,1,2,0:T(1,128)S(1)} fusion(f32[24,8,64,128]{3,2,1,0:T(8,128)S(1)} %bitcast.159, f32[24,128]{1,0:T(8,128)S(1)} %get-tuple-element.29, f32[24,8,64]{2,1,0:T(8,128)S(1)} %get-tuple-element.49, f32[24,8]{1,0:T(8,128)S(1)} %copy.86, f32[24,128]{1,0:T(8,128)S(1)} %get-tuple-element.26, f32[24,8,64]{2,1,0:T(8,128)S(1)} %get-tuple-element.51, ...), kind=kOutput, calls=%fused_computation.16 | convolution fusion | flops 28311552 | bytes 6598664 | tf_op jit(solution)/shard_map/rhpn,rn->rhp/dot_general | solution.py:78
  178.1 13.6 %fusion.2 = f32[24,1,8,64]{3,1,2,0:T(1,128)S(1)} fusion(f32[24,128]{1,0:T(8,128)S(1)} %get-tuple-element.28, f32[24,8,64]{2,1,0:T(8,128)S(1)} %get-tuple-element.48, f32[24,8]{1,0:T(8,128)S(1)} %copy.88, f32[24,8,64,128]{3,2,1,0:T(8,128)S(1)} %bitcast.159, f32[24,128]{1,0:T(8,128)S(1)} %get-tuple-element.29, f32[24,8,64]{2,1,0:T(8,128)S(1)} %get-tuple-element.49, ...), kind=kOutput, calls=%fused_computation.7 | convolution fusion | flops 33030144 | bytes 6721544 | tf_op jit(solution)/shard_map/rhpn,rn->rhp/dot_general | solution.py:78
  191.7 0.4 multiply_reduce_fusion.1
  192.1 0.1 reshape.411
  192.2 0.1 broadcast_multiply_fusion.4
  192.3 95.9 %all-reduce = (f32[24,4]{0,1:T(4,128)S(1)}, f32[24,4]{0,1:T(4,128)S(1)}, f32[24,4]{0,1:T(4,128)S(1)}, f32[24,4]{0,1:T(4,128)S(1)}) all-reduce(f32[24,4]{0,1:T(4,128)S(1)} %get-tuple-element.41, f32[24,4]{0,1:T(4,128)S(1)} %get-tuple-element.40, f32[24,4]{0,1:T(4,128)S(1)} %get-tuple-element.39, ...), channel_id=1, replica_groups=mesh['grp'=8,'tp'=16] {'tp'}, use_global_device_ids=true, to_apply=%region_1.2 | all-reduce | flops 384 | bytes 3072 | tf_op jit(solution)/shard_map/psum | solution.py:87
  288.2 0.1 multiply_reduce_fusion.7
  288.3 11.6 %convert_element_type.286 = f32[512,16,512]{2,0,1:T(8,128)} convert(bf16[512,16,512]{2,0,1:T(8,128)(2,1)} %all-to-all-done) | non-fusion elementwise | flops 4194304 | bytes 25165824 | tf_op jit(solution)/shard_map/convert_element_type | solution.py:48
  299.9 7.1 %copy.85 = f32[8,16,64,512]{3,2,1,0:T(8,128)S(1)} copy(f32[8,16,64,512]{3,2,0,1:T(8,128)} %bitcast.156) | data formatting | bytes 33554432 | tf_op jit(solution)/shard_map/convert_element_type | solution.py:48
  307.1 4.7 fusion
  311.7 3.2 copy-done
  315.0 3.3 fusion.39
  318.2 0.0 reduce-scatter.11.cloned.1.call-update
  318.3 0.0 reduce-scatter.9.cloned.1.call-start
  318.3 0.1 reshape.410
  318.4 6.6 %fusion.41 = f32[24,8192]{1,0:T(8,128)} fusion(bf16[8192,512]{1,0:T(8,128)(2,1)} %copy-done, f32[24,512]{1,0:T(8,128)S(1)} %reshape.410, f32[24]{0:T(128)S(1)} %add_rsqrt_fusion.1, f32[512]{0:T(512)S(1)} %copy-done.3, bf16[4,24,512]{2,1,0:T(8,128)(2,1)S(1)} %copy-done.2), kind=kOutput, calls=%fused_computation.68 | convolution fusion | flops 201437184 | bytes 9251328 | tf_op jit(solution)/shard_map/dot_general | solution.py:92
  325.0 0.0 reduce-scatter.7.cloned.1.call-start
  325.0 0.1 reshape.409
  325.1 6.6 %fusion.43 = f32[24,8192]{1,0:T(8,128)} fusion(bf16[8192,512]{1,0:T(8,128)(2,1)} %copy-done, f32[24,512]{1,0:T(8,128)S(1)} %reshape.409, f32[24]{0:T(128)S(1)} %add_rsqrt_fusion.2, f32[512]{0:T(512)S(1)} %copy-done.3, bf16[4,24,512]{2,1,0:T(8,128)(2,1)S(1)} %copy-done.2), kind=kOutput, calls=%fused_computation.69 | convolution fusion | flops 201437184 | bytes 9251328 | tf_op jit(solution)/shard_map/dot_general | solution.py:92
  331.8 0.0 reduce-scatter.5.cloned.1.call-start
  331.8 0.1 reshape.408
  331.9 6.7 %fusion.45 = f32[24,8192]{1,0:T(8,128)} fusion(bf16[8192,512]{1,0:T(8,128)(2,1)} %copy-done, f32[24,512]{1,0:T(8,128)S(1)} %reshape.408, f32[512]{0:T(512)S(1)} %copy-done.3, f32[24]{0:T(128)S(1)} %add_rsqrt_fusion.3, bf16[4,24,512]{2,1,0:T(8,128)(2,1)S(1)} %copy-done.2), kind=kOutput, calls=%fused_computation.70 | convolution fusion | flops 201437184 | bytes 9251328 | tf_op jit(solution)/shard_map/dot_general | solution.py:92
  338.7 48.5 %reduce-scatter.11.cloned.1.call-done = f32[24,512]{1,0:T(8,128)} async-done(((f32[24,8192]{1,0:T(8,128)}), f32[24,512]{1,0:T(8,128)}) %reduce-scatter.11.cloned.1.call-update) | async-done | bytes 49168 | tf_op jit(solution)/shard_map/reduce_scatter | solution.py:96
  387.2 0.8 convert_bitcast_fusion
  388.0 68.0 %reduce-scatter.9.cloned.1.call-done = f32[24,512]{1,0:T(8,128)} async-done(((f32[24,8192]{1,0:T(8,128)}), f32[24,512]{1,0:T(8,128)}) %reduce-scatter.9.cloned.1.call-update) | async-done | bytes 49168 | tf_op jit(solution)/shard_map/reduce_scatter | solution.py:96
  455.9 0.8 convert_bitcast_fusion.1
  456.7 67.8 %reduce-scatter.7.cloned.1.call-done = f32[24,512]{1,0:T(8,128)} async-done(((f32[24,8192]{1,0:T(8,128)}), f32[24,512]{1,0:T(8,128)}) %reduce-scatter.7.cloned.1.call-update) | async-done | bytes 49168 | tf_op jit(solution)/shard_map/reduce_scatter | solution.py:96
  524.5 0.8 convert_bitcast_fusion.2
  525.3 67.8 %reduce-scatter.5.cloned.1.call-done = f32[24,512]{1,0:T(8,128)} async-done(((f32[24,8192]{1,0:T(8,128)}), f32[24,512]{1,0:T(8,128)}) %reduce-scatter.5.cloned.1.call-update) | async-done | bytes 49168 | tf_op jit(solution)/shard_map/reduce_scatter | solution.py:96
  593.1 0.8 convert_bitcast_fusion.3
  593.9 0.7 pad_maximum_fusion
  (46 shorter events, 0.3 us)
Async XLA Ops:
  7.2 100.6 %all-gather.2.cloned.1.call-start = ((), (), s32[]{:S(2)}) async-start(), calls=%async_computation.5 | async-start | bytes 9437184 | tf_op jit(solution)/shard_map/all_gather | solution.py:40
  132.1 7.7 %copy-start.2 = (bf16[4,24,512]{2,1,0:T(8,128)(2,1)S(1)}, bf16[4,24,512]{2,1,0:T(8,128)(2,1)}, u32[]{:S(2)}) copy-start(bf16[4,24,512]{2,1,0:T(8,128)(2,1)} %param.18) | copy-start | bytes 294916
  132.1 7.8 %copy-start.4 = (bf16[4,24,512]{2,1,0:T(8,128)(2,1)S(1)}, bf16[4,24,512]{2,1,0:T(8,128)(2,1)}, u32[]{:S(2)}) copy-start(bf16[4,24,512]{2,1,0:T(8,128)(2,1)} %param.19) | copy-start | bytes 294916
  132.1 7.9 %copy-start.6 = (bf16[4,24,512]{2,1,0:T(8,128)(2,1)S(1)}, bf16[4,24,512]{2,1,0:T(8,128)(2,1)}, u32[]{:S(2)}) copy-start(bf16[4,24,512]{2,1,0:T(8,128)(2,1)} %param.17) | copy-start | bytes 294916
  132.1 8.0 %copy-start.7 = (bf16[4,24,8]{1,2,0:T(8,128)(2,1)S(1)}, bf16[4,24,8]{1,2,0:T(8,128)(2,1)}, u32[]{:S(2)}) copy-start(bf16[4,24,8]{1,2,0:T(8,128)(2,1)} %param.21) | copy-start | bytes 4612
  132.1 8.0 %copy-start.8 = (f32[8]{0:T(128)S(1)}, f32[8]{0:T(128)}, u32[]{:S(2)}) copy-start(f32[8]{0:T(128)} %param.23) | copy-start | bytes 100
  132.1 8.0 %copy-start.9 = (f32[8]{0:T(128)S(1)}, f32[8]{0:T(128)}, u32[]{:S(2)}) copy-start(f32[8]{0:T(128)} %param.22) | copy-start | bytes 100
  132.1 8.8 %copy-start.5 = (bf16[4,24,512]{2,1,0:T(8,128)(2,1)S(1)}, bf16[4,24,512]{2,1,0:T(8,128)(2,1)}, u32[]{:S(2)}) copy-start(bf16[4,24,512]{2,1,0:T(8,128)(2,1)} %param.20) | copy-start | bytes 294916
  132.1 156.2 %all-to-all-start = ((bf16[512,16,512]{2,0,1:T(8,128)(2,1)}), bf16[512,16,512]{2,0,1:T(8,128)(2,1)}, u32[]{:S(2)}, u32[]{:S(2)}) async-start(bf16[512,16,512]{2,0,1:T(8,128)(2,1)} %copy.84), calls=%async_computation | async-start | bytes 16777216 | tf_op jit(solution)/shard_map/all_to_all | solution.py:41
  139.6 247.6 %reduce-scatter.11.cloned.1.call-start = ((), (), s32[]{:S(2)}) async-start(), calls=%async_computation.9 | async-start | bytes 835584 | tf_op jit(solution)/shard_map/reduce_scatter | solution.py:96
  141.4 17.6 %slice-start = ((s8[6291456]{0:T(1024)(128)(4,1)}), s8[4194304]{0:T(1024)(128)(4,1)S(1)}, s32[]{:S(2)}) async-start(s8[6291456]{0:T(1024)(128)(4,1)} %bitcast.158), calls=%async_computation.10 | async-start | bytes 8388608
  141.7 17.4 %slice-start.1 = ((s8[6291456]{0:T(1024)(128)(4,1)}), s8[2097152]{0:T(1024)(128)(4,1)S(1)}, s32[]{:S(2)}) async-start(s8[6291456]{0:T(1024)(128)(4,1)} %bitcast.158), calls=%async_computation.11 | async-start | bytes 4194304
  151.6 15.6 %copy-start.1 = (f32[24,8,64,128]{3,2,1,0:T(8,128)}, f32[24,8,64,128]{3,2,1,0:T(8,128)S(1)}, u32[]{:S(2)}) copy-start(f32[24,8,64,128]{3,2,1,0:T(8,128)S(1)} %multiply_add_fusion) | copy-start | bytes 18874372
  178.1 13.6 %copy-start.10 = (f32[8]{0:T(128)S(1)}, f32[8]{0:T(128)}, u32[]{:S(2)}) copy-start(f32[8]{0:T(128)} %param.24) | copy-start | bytes 100
  288.3 18.7 %slice-start.2 = ((s8[8388608]{0:T(1024)(128)(4,1)}), s8[4194304]{0:T(1024)(128)(4,1)S(1)}, s32[]{:S(2)}) async-start(s8[8388608]{0:T(1024)(128)(4,1)} %bitcast.161), calls=%async_computation.12 | async-start | bytes 8388608
  299.9 7.1 %slice-start.3 = ((s8[8388608]{0:T(1024)(128)(4,1)}), s8[4194304]{0:T(1024)(128)(4,1)S(1)}, s32[]{:S(2)}) async-start(s8[8388608]{0:T(1024)(128)(4,1)} %bitcast.161), calls=%async_computation.13 | async-start | bytes 8388608
  307.0 7.9 %copy-start.3 = (f32[512]{0:T(512)S(1)}, f32[512]{0:T(512)}, u32[]{:S(2)}) copy-start(f32[512]{0:T(512)} %param.25) | copy-start | bytes 6148
  311.7 3.2 copy-start
  318.3 137.7 %reduce-scatter.9.cloned.1.call-start = ((), (), s32[]{:S(2)}) async-start(), calls=%async_computation.8 | async-start | bytes 835584 | tf_op jit(solution)/shard_map/reduce_scatter | solution.py:96
  325.0 199.5 %reduce-scatter.7.cloned.1.call-start = ((), (), s32[]{:S(2)}) async-start(), calls=%async_computation.7 | async-start | bytes 835584 | tf_op jit(solution)/shard_map/reduce_scatter | solution.py:96
  331.8 261.3 %reduce-scatter.5.cloned.1.call-start = ((), (), s32[]{:S(2)}) async-start(), calls=%async_computation.6 | async-start | bytes 835584 | tf_op jit(solution)/shard_map/reduce_scatter | solution.py:96
Sparse Core Ops, SparseCore 0:
  12.6 95.1 all-gather.1
  318.4 68.7 reduce-scatter.10
  390.9 64.9 reduce-scatter.8
  459.5 64.9 reduce-scatter.6
  528.1 64.9 reduce-scatter.4
where the time goes:
time: 603 us; the launch traced here: 601 us
  waiting for transfers between devices  347 us (58%)
  blocking collectives  95.9 us (16%)
  matrix products  63.2 us (10%)
  local copies, waits for them, and re-layouts  37 us (6%)
  other arithmetic  35.6 us (6%)
  between operations  14.1 us (2%)
  starting transfers between devices  7.79 us (1%)
    reduce_scatter x4, waiting for transfers between devices, local(): lax.psum_scatter(partial_value, 'tp', scatter_dimension=1, tiled=True)  252 us
    psum x1, blocking collectives, local(): lax.psum(jnp.sum(gated_value * gated_value, axis=1)[:, None] * selector,...  95.9 us
    all_gather x1, waiting for transfers between devices, local(): grouped_rows = lax.all_gather(delta_part, 'grp', axis=0, tiled=True)  95.3 us
    dot_general x4, matrix products, local(): jnp.einsum('rhpn,rn->rhp', local_carried, c_local[step_index], precision=...  40 us
    dot_general x4, matrix products, local(): lax.dot_general(normed, new_weight, (((1,), (1,)), ((), ())), preferred_e...  23.2 us
    all_to_all x1, local copies, waits for them, and re-layouts, local(): lax.all_to_all(grouped_rows, 'tp', split_axis=1, concat_axis=0, tiled=True)  12.3 us
  transfers between devices with their start and end apart: 6, of which 5 were waited for; matrix products, arithmetic and copies ran while one was open for 12% of the time, Pallas kernels for 0%

commit v1 on v0

v1 whole, which is shorter than its diff:
```python
import functools

import jax
import jax.numpy as jnp
from jax import lax
from jax.experimental import pallas as pl
from jax.experimental.pallas import tpu as pltpu
from jax.sharding import PartitionSpec as P

MESH = pl.DeviceIdType.MESH
F32 = jnp.float32
BF16 = jnp.bfloat16
STEPS = 4
ROWS = 24
ALL = STEPS * ROWS
LOCAL = 512
STATE = 128
GROUP_WIDTH = 2048
ROW_BLOCK = 4
CONTRACT_LAST = (((1,), (1,)), ((), ()))
CONTRACT_FIRST = (((0,), (0,)), ((), ()))


def split3(value):
    first = value.astype(BF16)
    rest = value - first.astype(F32)
    second = rest.astype(BF16)
    third = (rest - second.astype(F32)).astype(BF16)
    return first, second, third


def expand_heads(value, spread):
    parts = split3(value)
    total = jnp.dot(parts[2], spread, preferred_element_type=F32)
    total = total + jnp.dot(parts[1], spread, preferred_element_type=F32)
    return total + jnp.dot(parts[0], spread, preferred_element_type=F32)


def put(ref, first, value):
    for j in range(value.shape[1] // 128):
        ref[j, first:first + value.shape[0], :] = value[:, j * 128:(j + 1) * 128]


def pick_rows(ref, row, count):
    return jnp.concatenate(
        [ref[j, pl.ds(row, count, stride=ROWS), :] for j in range(ref.shape[0])], axis=1
    )


def step_kernel(
    state_ref, x_ref, z_ref, b_ref, c_ref, dt_ref, bias_ref, rate_ref, skip_ref, gain_ref,
    final_ref, act_ref, square_ref,
    left_rows, right_rows, read_rows, read_state, decay_rows, direct_rows,
):
    at = pl.program_id(0)
    group = lax.axis_index("tp") // 4
    lanes = pl.ds(pl.multiple_of(group * STATE, STATE), STATE)

    @pl.when(at == 0)
    def _():
        heads = bias_ref.shape[1]
        head_of = lax.broadcasted_iota(jnp.int32, (heads, LOCAL), 1) // (LOCAL // heads)
        spread = (head_of == lax.broadcasted_iota(jnp.int32, (heads, LOCAL), 0)).astype(BF16)
        raw = jnp.concatenate([dt_ref[s].astype(F32) for s in range(STEPS)], axis=0)
        raw = raw + bias_ref[...]
        soft = jnp.maximum(raw, 0.0) + jnp.log1p(jnp.exp(-jnp.abs(raw)))
        rate = expand_heads(jnp.broadcast_to(rate_ref[...], (8, heads)), spread)[0:1]
        skip = expand_heads(jnp.broadcast_to(skip_ref[...], (8, heads)), spread)[0:1]
        size = expand_heads(soft, spread)
        sizes = [size[s * ROWS:(s + 1) * ROWS] for s in range(STEPS)]
        logs = []
        for s in range(STEPS):
            own = sizes[s] * rate
            logs.append(own if s == 0 else logs[-1] + own)
        xs = [x_ref[s].astype(F32) for s in range(STEPS)]
        bs = [b_ref[s, :, lanes].astype(F32) for s in range(STEPS)]
        cs = [c_ref[s, :, lanes].astype(F32) for s in range(STEPS)]
        for s in range(STEPS):
            decay_rows[s * ROWS:(s + 1) * ROWS, :] = jnp.exp(-logs[s])
            direct = skip * xs[s]
            for u in range(s + 1):
                coef = sizes[u] if u == s else sizes[u] * jnp.exp(logs[u] - logs[s])
                term = coef * xs[u]
                direct = direct + term * jnp.sum(bs[u] * cs[s], axis=1, keepdims=True)
                if s == STEPS - 1:
                    high = term.astype(BF16).astype(F32)
                    put(left_rows, u * ROWS, high)
                    put(left_rows, (4 + u) * ROWS, term - high)
            direct_rows[s * ROWS:(s + 1) * ROWS, :] = direct
        last = decay_rows[3 * ROWS:4 * ROWS, :]
        for at_row, part in enumerate(split3(last)):
            put(left_rows, (8 + at_row) * ROWS, part.astype(F32))
        put(left_rows, 11 * ROWS, jnp.zeros((5 * ROWS, LOCAL), F32))
        right_rows[...] = jnp.zeros(right_rows.shape, F32)
        read_rows[...] = jnp.zeros(read_rows.shape, F32)
        for s in range(STEPS):
            right_rows[0, s * ROWS:(s + 1) * ROWS, :] = bs[s]
            right_rows[0, (4 + s) * ROWS:(5 + s) * ROWS, :] = bs[s]
            read_rows[0, s * ROWS:(s + 1) * ROWS, :] = cs[s]
        right_rows[1, 8 * ROWS:11 * ROWS, :] = jnp.ones((3 * ROWS, STATE), F32)

    for i in range(ROW_BLOCK):
        row = at * ROW_BLOCK + i
        held = state_ref[i].reshape(LOCAL, STATE)
        high = held.astype(BF16)
        low = (held - high.astype(F32)).astype(BF16)
        both = jnp.concatenate([high, low], axis=1)
        reader = pick_rows(read_rows, row, 8).astype(BF16)
        reader = jnp.concatenate([reader, reader], axis=1)
        read = lax.dot_general(reader, both, CONTRACT_LAST, preferred_element_type=F32)
        for j in range(LOCAL // 128):
            read_state[j, pl.ds(row, 8, stride=ROWS), :] = read[:, j * 128:(j + 1) * 128]
        left = pick_rows(left_rows, row, 16).astype(BF16)
        right = pick_rows(right_rows, row, 16).astype(BF16)
        update = lax.dot_general(left, right, CONTRACT_FIRST, preferred_element_type=F32)
        final_ref[i] = (update[:, STATE:] * held + update[:, :STATE]).reshape(final_ref.shape[1:])

    @pl.when(at == pl.num_programs(0) - 1)
    def _():
        z = jnp.concatenate([z_ref[s].astype(F32) for s in range(STEPS)], axis=0)
        read = jnp.concatenate([read_state[j, 0:ALL, :] for j in range(LOCAL // 128)], axis=1)
        read_out = decay_rows[...] * read + direct_rows[...]
        gated = read_out * (z / (1.0 + jnp.exp(-z)))
        act_ref[...] = (gated * gain_ref[...]).astype(BF16)
        total = jnp.sum(gated * gated, axis=1, keepdims=True)
        total = jnp.concatenate([total, jnp.zeros((128 - ALL, 1), F32)], axis=0)
        square_ref[...] = jnp.transpose(jnp.broadcast_to(total, (128, 128)))[0:8]


def run_steps(state_in, x_in, z_in, b_in, c_in, dt_in, dt_bias, a_rate, skip_gain, norm_gain):
    whole = lambda a: pl.BlockSpec(a.shape, lambda i, nd=a.ndim: (0,) * nd)
    vectors = [v.reshape(1, -1) for v in (dt_bias, a_rate, skip_gain, norm_gain)]
    block = pl.BlockSpec((ROW_BLOCK,) + state_in.shape[1:], lambda i: (i, 0, 0, 0))
    others = [x_in, z_in, b_in, c_in, dt_in] + vectors
    return pl.pallas_call(
        step_kernel,
        grid=(ROWS // ROW_BLOCK,),
        out_shape=(
            jax.ShapeDtypeStruct(state_in.shape, F32),
            jax.ShapeDtypeStruct((ALL, LOCAL), BF16),
            jax.ShapeDtypeStruct((8, 128), F32),
        ),
        in_specs=[block] + [whole(a) for a in others],
        out_specs=(
            block,
            pl.BlockSpec((ALL, LOCAL), lambda i: (0, 0)),
            pl.BlockSpec((8, 128), lambda i: (0, 0)),
        ),
        scratch_shapes=[
            pltpu.VMEM((LOCAL // 128, 16 * ROWS, 128), F32),
            pltpu.VMEM((2, 16 * ROWS, STATE), F32),
            pltpu.VMEM((1, 8 * ROWS, STATE), F32),
            pltpu.VMEM((LOCAL // 128, 8 * ROWS, 128), F32),
            pltpu.VMEM((ALL, LOCAL), F32),
            pltpu.VMEM((ALL, LOCAL), F32),
        ],
        compiler_params=pltpu.CompilerParams(vmem_limit_bytes=60 * 1024 * 1024),
        cost_estimate=pl.CostEstimate(flops=10**8, bytes_accessed=13 * 10**6, transcendentals=0),
    )(state_in, *others)


OFFSETS = ((2, 1), (1, 1), (3, 1), (2, 0), (1, 0), (3, 0), (0, 1), (0, 0))
GATHER = ((0, 2), (1, 2), (0, 1), (0, 3), (1, 1), (1, 3), (1, 0))


def mix_kernel(
    codes_ref, exps_ref, old_ref, act_ref, square_ref, out_ref,
    codes, delta, weight, arrived, acts, parts, sums, squares,
    codes_sem, own_sem, old_send, old_recv, delta_send, delta_recv,
    act_send, act_recv, fwd_send, fwd_recv, own_act_sem,
    part_send, part_recv, square_send, square_recv,
):
    grp, tp = lax.axis_index("grp"), lax.axis_index("tp")
    z_lo, x = grp // 4, grp % 4
    y, z_hi, core = tp // 4, (tp // 2) % 2, tp % 2
    other = 1 - core
    chip = tp // 2
    partner = (grp, tp - core + other)
    mine = chip == grp
    crossed = chip == (1 - z_lo) * 4 + x

    def place(lo, xx, yy, hi, cc):
        return (lo * 4 + xx, yy * 4 + hi * 2 + cc)

    for k in range(8):
        dy, dz = OFFSETS[k]
        column = ((y + dy) % 4) * 2 + (z_hi + dz) % 2
        pltpu.make_async_copy(
            codes_ref.at[:, pl.ds(pl.multiple_of(column * 1024, 1024), 1024)], codes.at[k], codes_sem.at[k]
        ).start()

    barrier = pltpu.get_barrier_semaphore()

    def greet(where):
        pl.semaphore_signal(barrier, inc=1, device_id=where, device_id_type=MESH)

    greet(partner)
    for cc in range(2):
        for yl in range(2):
            for dz in range(2):
                where = place((z_lo + dz) % 2, x, 2 * core + yl, (z_hi + dz) % 2, cc)
                if dz == 0:
                    @pl.when(jnp.logical_not((cc == core) & (2 * core + yl == y)))
                    def _():
                        greet(where)
                else:
                    greet(where)
    for dl, dx in GATHER:
        greet(((z_lo + dl) % 2 * 4 + (x + dx) % 4, tp))
    for dt in range(1, 16):
        greet((grp, (tp + dt) % 16))
    for lo in range(2):
        for yy in range(4):
            for hi in range(2):
                where = place(lo, chip % 4, yy, hi, core)

                @pl.when(jnp.logical_not((where[0] == grp) & (where[1] == tp)))
                def _():
                    greet(where)
    own_delta = core == y // 2
    expected = (
        1 + 8 - own_delta.astype(jnp.int32) + 7 + 15 + 16 - mine.astype(jnp.int32) - crossed.astype(jnp.int32)
    )
    pl.semaphore_wait(barrier, expected)

    def act_copy(k):
        dl, dx = GATHER[k]
        return pltpu.make_async_remote_copy(
            src_ref=act_ref, dst_ref=acts.at[grp, :, pl.ds(pl.multiple_of(core * LOCAL, LOCAL), LOCAL)],
            send_sem=act_send.at[k], recv_sem=act_recv.at[k],
            device_id=((z_lo + dl) % 2 * 4 + (x + dx) % 4, tp), device_id_type=MESH,
        )

    def fwd_copy(k):
        if k == 7:
            source, slot = act_ref, grp
        else:
            dl, dx = GATHER[k]
            slot = (z_lo + dl) % 2 * 4 + (x + 4 - dx) % 4
            source = acts.at[slot, :, pl.ds(pl.multiple_of(core * LOCAL, LOCAL), LOCAL)]
        return pltpu.make_async_remote_copy(
            src_ref=source, dst_ref=acts.at[slot, :, pl.ds(pl.multiple_of(core * LOCAL, LOCAL), LOCAL)],
            send_sem=fwd_send.at[k], recv_sem=fwd_recv.at[k],
            device_id=partner, device_id_type=MESH,
        )

    def square_copy(k):
        return pltpu.make_async_remote_copy(
            src_ref=square_ref, dst_ref=squares.at[tp],
            send_sem=square_send.at[k], recv_sem=square_recv.at[k],
            device_id=(grp, (tp + k + 1) % 16), device_id_type=MESH,
        )

    def feature_row(slab, cc):
        dz, yl = slab // 2, slab % 2
        lo, hi = (z_lo + dz) % 2, (z_hi + dz) % 2
        row = ((lo * 4 + x) * 2 + cc) * 512 + yl * 256 + hi * 128
        return pl.ds(pl.multiple_of(row, 128), 128)

    def own_copy(slab):
        return pltpu.make_async_copy(
            old_ref.at[feature_row(slab, core)],
            weight.at[pl.ds(slab * 128, 128), pl.ds(pl.multiple_of(core * LOCAL, LOCAL), LOCAL)],
            own_sem.at[slab],
        )

    def old_copy(slab):
        return pltpu.make_async_remote_copy(
            src_ref=old_ref.at[feature_row(slab, other)],
            dst_ref=weight.at[pl.ds(slab * 128, 128), pl.ds(pl.multiple_of(core * LOCAL, LOCAL), LOCAL)],
            send_sem=old_send.at[slab], recv_sem=old_recv.at[slab],
            device_id=partner, device_id_type=MESH,
        )

    def delta_copy(k):
        dy, dz = OFFSETS[k]
        first = pl.multiple_of(dz * 256 + (y % 2) * 128 + core * 64, 64)
        slot = dz * 4 + (y % 2) * 2 + core
        return pltpu.make_async_remote_copy(
            src_ref=delta.at[k], dst_ref=arrived.at[pl.ds(first, 64)],
            send_sem=delta_send.at[k], recv_sem=delta_recv.at[slot],
            device_id=place((z_lo + dz) % 2, x, (y + dy) % 4, (z_hi + dz) % 2, y // 2), device_id_type=MESH,
        )

    def delta_self():
        first = pl.multiple_of((y % 2) * 128 + core * 64, 64)
        return pltpu.make_async_copy(
            delta.at[7], arrived.at[pl.ds(first, 64)], delta_recv.at[(y % 2) * 2 + core]
        )

    scale = jnp.where(
        exps_ref[...] == -14, 2.0**-14, jnp.where(exps_ref[...] == -13, 2.0**-13, 2.0**-12)
    ).astype(BF16)
    block_at = lax.broadcasted_iota(jnp.int32, (64, 1024), 0)
    lane_block = lax.broadcasted_iota(jnp.int32, (64, 1024), 1) // 128
    for k in range(8):
        dy, dz = OFFSETS[k]
        column = ((y + dy) % 4) * 2 + (z_hi + dz) % 2
        pltpu.make_async_copy(codes.at[k], codes.at[k], codes_sem.at[k]).wait()
        pick = (block_at == lane_block + column * 8).astype(BF16)
        wide = jnp.dot(scale, pick, preferred_element_type=F32)
        delta[k] = (codes[k].astype(F32) * wide).astype(BF16)
        if k < 7:
            delta_copy(k).start()
        else:
            @pl.when(own_delta)
            def _():
                delta_self().start()

            @pl.when(jnp.logical_not(own_delta))
            def _():
                delta_copy(7).start()
        if k < 7:
            act_copy(k).start()
    fwd_copy(7).start()
    own_act = pltpu.make_async_copy(
        act_ref, acts.at[grp, :, pl.ds(pl.multiple_of(core * LOCAL, LOCAL), LOCAL)], own_act_sem
    )
    own_act.start()
    for slab in range(4):
        own_copy(slab).start()
        old_copy(slab).start()
    for k in range(15):
        square_copy(k).start()
    squares[tp] = square_ref[...]

    for k in range(7):
        act_copy(k).wait_recv()
        fwd_copy(k).start()
    own_act.wait()
    for k in range(8):
        fwd_copy(k).wait_recv()

    def part_copy(half, g):
        lo = (z_lo + half) % 2
        dest = (g, (lo * 4 + x) * 2 + core)
        slot = ((z_hi + half) % 2) * 8 + y * 2 + half
        remote = lambda: pltpu.make_async_remote_copy(
            src_ref=parts.at[half * 8 + g], dst_ref=sums.at[slot],
            send_sem=part_send.at[half * 8 + g], recv_sem=part_recv.at[slot],
            device_id=dest, device_id_type=MESH,
        )
        local = lambda: pltpu.make_async_copy(parts.at[half * 8 + g], sums.at[slot], part_recv.at[slot])
        here = (dest[0] == grp) & (dest[1] == tp)
        return remote, local, here

    for half in range(2):
        for slab in (half * 2, half * 2 + 1):
            own_copy(slab).wait()
            old_copy(slab).wait_recv()
        for slot in range(half * 4, half * 4 + 4):
            rows = arrived.at[pl.ds(slot * 64, 64)]
            pltpu.make_async_copy(rows, rows, delta_recv.at[slot]).wait()
        span = slice(half * 256, half * 256 + 256)
        fresh = (weight[span, :].astype(F32) + arrived[span, :].astype(F32)).astype(BF16)
        for quarter in range(4):
            lhs = acts[quarter * 2:quarter * 2 + 2].reshape(2 * ALL, 1024)
            got = lax.dot_general(lhs, fresh, CONTRACT_LAST, preferred_element_type=F32)
            for part in range(2):
                g = quarter * 2 + part
                parts[half * 8 + g] = got[part * ALL:(part + 1) * ALL].astype(BF16)
                remote, local, here = part_copy(half, g)

                @pl.when(here)
                def _():
                    local().start()

                @pl.when(jnp.logical_not(here))
                def _():
                    remote().start()

    for k in range(15):
        square_copy(k).wait_recv()
    by_group = [
        squares[4 * yy] + squares[4 * yy + 1] + squares[4 * yy + 2] + squares[4 * yy + 3] for yy in range(4)
    ]
    factors = []
    for yy in range(4):
        inverse = lax.rsqrt(by_group[yy] * (1.0 / GROUP_WIDTH) + 1e-05)
        tall = jnp.concatenate([inverse] * 16, axis=0)
        factors.append(jnp.transpose(tall)[0:ALL, 0:1])
    for hi in range(2):
        total = None
        for yy in range(4):
            pair = None
            for half in range(2):
                slot = hi * 8 + yy * 2 + half
                pltpu.make_async_copy(sums.at[slot], sums.at[slot], part_recv.at[slot]).wait()
                value = sums[slot].astype(F32)
                pair = value if pair is None else pair + value
            pair = pair * factors[yy]
            total = pair if total is None else total + pair
        for s in range(STEPS):
            for yl in range(2):
                out_ref[s, :, yl * 256 + hi * 128:yl * 256 + hi * 128 + 128] = total[
                    s * ROWS:(s + 1) * ROWS, yl * 128:(yl + 1) * 128
                ].astype(BF16)

    for k in range(7):
        delta_copy(k).wait_send()
        act_copy(k).wait_send()
    for k in range(8):
        fwd_copy(k).wait_send()

    @pl.when(jnp.logical_not(own_delta))
    def _():
        delta_copy(7).wait_send()
    for slab in range(4):
        old_copy(slab).wait_send()
    for k in range(15):
        square_copy(k).wait_send()
    for half in range(2):
        for g in range(8):
            remote, local, here = part_copy(half, g)

            @pl.when(jnp.logical_not(here))
            def _():
                remote().wait_send()


def run_mix(delta_codes, delta_exps, old_weight, act, square):
    vmem = pl.BlockSpec(memory_space=pltpu.VMEM)
    hbm = pl.BlockSpec(memory_space=pltpu.HBM)
    dma = pltpu.SemaphoreType.DMA
    return pl.pallas_call(
        mix_kernel,
        out_shape=jax.ShapeDtypeStruct((STEPS, ROWS, LOCAL), BF16),
        in_specs=[hbm, vmem, hbm, vmem, vmem],
        out_specs=vmem,
        scratch_shapes=[
            pltpu.VMEM((8, 64, 1024), jnp.int32),
            pltpu.VMEM((8, 64, 1024), BF16),
            pltpu.VMEM((512, 1024), BF16),
            pltpu.VMEM((512, 1024), BF16),
            pltpu.VMEM((8, ALL, 1024), BF16),
            pltpu.VMEM((16, ALL, 256), BF16),
            pltpu.VMEM((16, ALL, 256), BF16),
            pltpu.VMEM((16, 8, 128), F32),
            dma((8,)), dma((4,)), dma((4,)), dma((4,)), dma((8,)), dma((8,)),
            dma((7,)), dma((7,)), dma((8,)), dma((8,)), dma,
            dma((16,)), dma((16,)), dma((15,)), dma((15,)),
        ],
        compiler_params=pltpu.CompilerParams(
            collective_id=0, has_side_effects=True, vmem_limit_bytes=60 * 1024 * 1024
        ),
        cost_estimate=pl.CostEstimate(flops=8 * 10**8, bytes_accessed=4 * 10**6, transcendentals=0),
    )(delta_codes, delta_exps, old_weight, act, square)


def local(
    old_weight, delta_codes, delta_exps, state_in, x_in, z_in, b_in, c_in, dt_in,
    dt_bias, a_rate, skip_gain, norm_gain,
):
    final_state, act, square = run_steps(
        state_in, x_in, z_in, b_in, c_in, dt_in, dt_bias, a_rate, skip_gain, norm_gain
    )
    mixed = run_mix(delta_codes, delta_exps, old_weight, act, square)
    return mixed, final_state


def solution(mesh):
    return jax.shard_map(
        local,
        mesh=mesh,
        in_specs=(
            P(None, "tp"),
            P(("grp", "tp"), None),
            P(("grp", "tp"), None),
            P("grp", "tp", None, None),
            P(None, "grp", "tp"),
            P(None, "grp", "tp"),
            P(None, "grp", None),
            P(None, "grp", None),
            P(None, "grp", "tp"),
            P("tp"),
            P("tp"),
            P("tp"),
            P("tp"),
        ),
        out_specs=(P(None, "grp", "tp"), P("grp", "tp", None, None)),
        check_vma=False,
    )
```

time: 603 us -> 53.2 us (0.09)
  the two profiles are of different devices: /device:TPU:1 before, /device:TPU:40 now
where the time goes in v1:
time: 53.2 us; the launch traced here: 52.8 us
  Pallas kernels  49.3 us (93%)
  local copies, waits for them, and re-layouts  2.92 us (5%)
  between operations  0.64 us (1%)
    pallas_call x1, Pallas kernels, run_mix(): pl.pallas_call(mix_kernel, out_shape=jax.ShapeDtypeStruct((STEPS, ROWS, L...  40.2 us
    pallas_call x1, Pallas kernels, run_steps(): pl.pallas_call(step_kernel, grid=(ROWS // ROW_BLOCK,), out_shape=(jax.Sha...  9.09 us
    unnamed x2, local copies, waits for them, and re-layouts  2.92 us

profile of v1, /device:TPU:40, one launch (start us, length us, event | category | flops | bytes accessed | tf_op | source)
XLA Modules:
  0.0 52.8 jit_solution(3113933591993153662)
XLA Ops:
  0.6 1.4 %copy.15.dt_ref = bf16[4,24,8]{2,1,0:T(8,128)(2,1)} copy(bf16[4,24,8]{1,2,0:T(8,128)(2,1)} %param.21) | data formatting | bytes 3072 | tf_op args[8]
  2.0 9.1 %shard_map.140 = (f32[24,8,64,128]{3,2,1,0:T(8,128)}, bf16[96,512]{1,0:T(8,128)(2,1)}, f32[8,128]{1,0:T(8,128)}) custom-call(f32[24,8,64,128]{3,2,1,0:T(8,128)} %state_ref.1, bf16[4,24,512]{2,1,0:T(8,128)(2,1)} %x_ref.1, bf16[4,24,512]{2,1,0:T(8,128)(2,1)} %z_ref.1, bf16[4,24,512]{2,1,0:T(8,128)(2,1)} %b_ref.1, bf16[4,24,512]{2,1,0:T(8,128)(2,1)} %c_ref.1, ...), custom_call_target="tpu_custom_call" | custom-call | flops 100000000 | bytes 13000000 | tf_op jit(solution)/shard_map/pallas_call | solution.py:135
  11.1 40.2 %shard_map.141 = bf16[4,24,512]{2,1,0:T(8,128)(2,1)} custom-call(s32[64,8192]{1,0:T(8,128)} %codes_ref.1, s32[64,64]{1,0:T(8,128)} %exps_ref.1, bf16[8192,512]{1,0:T(8,128)(2,1)} %old_ref.1, bf16[96,512]{1,0:T(8,128)(2,1)} %get-tuple-element.5.act_ref, f32[8,128]{1,0:T(8,128)} %get-tuple-element.6.square_ref), custom_call_target="tpu_custom_call" | custom-call | flops 800000000 | bytes 4000000 | tf_op jit(solution)/shard_map/pallas_call | solution.py:425
  51.3 1.5 %copy.17 = bf16[4,24,512]{2,1,0:T(8,128)(2,1)} copy(bf16[4,24,512]{2,1,0:T(8,128)(2,1)} %shard_map.141) | data formatting | bytes 196608

commit v2 on v1

v2 whole, which is shorter than its diff:
```python
import functools

import jax
import jax.numpy as jnp
from jax import lax
from jax.experimental import pallas as pl
from jax.experimental.pallas import tpu as pltpu
from jax.sharding import PartitionSpec as P

MESH = pl.DeviceIdType.MESH
F32 = jnp.float32
BF16 = jnp.bfloat16
STEPS = 4
ROWS = 24
ALL = STEPS * ROWS
LOCAL = 512
STATE = 128
GROUP_WIDTH = 2048
CHUNKS = 3
CHUNK_ROWS = ROWS // CHUNKS
SENT_ROWS = STEPS * CHUNK_ROWS
HEADS = 8
CONTRACT_LAST = (((1,), (1,)), ((), ()))
CONTRACT_FIRST = (((0,), (0,)), ((), ()))


def split3(value):
    first = value.astype(BF16)
    rest = value - first.astype(F32)
    second = rest.astype(BF16)
    third = (rest - second.astype(F32)).astype(BF16)
    return first, second, third


def expand_heads(value, spread):
    parts = split3(value)
    total = jnp.dot(parts[2], spread, preferred_element_type=F32)
    total = total + jnp.dot(parts[1], spread, preferred_element_type=F32)
    return total + jnp.dot(parts[0], spread, preferred_element_type=F32)


def put(ref, first, value):
    for j in range(value.shape[1] // 128):
        ref[j, first:first + value.shape[0], :] = value[:, j * 128:(j + 1) * 128]


def pick_rows(ref, row, count):
    return jnp.concatenate(
        [ref[j, pl.ds(row, count, stride=ROWS), :] for j in range(ref.shape[0])], axis=1
    )


UNROLL = 4
OFFSETS = ((2, 1), (1, 1), (3, 1), (2, 0), (1, 0), (3, 0), (0, 1), (0, 0))
GATHER = ((0, 2), (1, 2), (0, 1), (0, 3), (1, 1), (1, 3), (1, 0))


def mix_kernel(
    codes_ref, exps_ref, old_ref, state_ref, x_ref, z_ref, b_ref, c_ref, dt_ref,
    bias_ref, rate_ref, skip_ref, gain_ref,
    held, sums, squares,
    exps, xs_in, zs_in, bs_in, cs_in, dts_in, bias_in, rate_in, skip_in, gain_in,
    left_rows, right_rows, read_rows, read_state, decay_rows, direct_rows, square_rows,
    codes, delta, weight, arrived, acts, parts,
    small_sem, state_sem, codes_sem, own_sem, old_send, old_recv, delta_send, delta_recv,
    act_send, act_recv, fwd_send, fwd_recv, part_send, part_recv, square_send, square_recv,
):
    grp, tp = lax.axis_index("grp"), lax.axis_index("tp")
    z_lo, x = grp // 4, grp % 4
    y, z_hi, core = tp // 4, (tp // 2) % 2, tp % 2
    other = 1 - core
    chip = tp // 2
    partner = (grp, tp - core + other)
    mine = chip == grp
    crossed = chip == (1 - z_lo) * 4 + x

    def place(lo, xx, yy, hi, cc):
        return (lo * 4 + xx, yy * 4 + hi * 2 + cc)

    for k in range(8):
        dy, dz = OFFSETS[k]
        column = ((y + dy) % 4) * 2 + (z_hi + dz) % 2
        pltpu.make_async_copy(
            codes_ref.at[:, pl.ds(pl.multiple_of(column * 1024, 1024), 1024)], codes.at[k], codes_sem.at[k]
        ).start()

    small = [
        (exps_ref, exps), (dt_ref, dts_in), (bias_ref, bias_in), (rate_ref, rate_in), (skip_ref, skip_in),
        (x_ref, xs_in), (b_ref, bs_in), (c_ref, cs_in), (z_ref, zs_in), (gain_ref, gain_in),
    ]

    def small_copy(k):
        return pltpu.make_async_copy(small[k][0], small[k][1], small_sem.at[k])

    def state_copy(c):
        span = pl.ds(c * CHUNK_ROWS, CHUNK_ROWS)
        return pltpu.make_async_copy(state_ref.at[span], held.at[span], state_sem.at[c])

    for k in range(len(small)):
        small_copy(k).start()
    for c in range(CHUNKS):
        state_copy(c).start()

    barrier = pltpu.get_barrier_semaphore()

    def greet(where):
        pl.semaphore_signal(barrier, inc=1, device_id=where, device_id_type=MESH)

    greet(partner)
    for cc in range(2):
        for yl in range(2):
            for dz in range(2):
                where = place((z_lo + dz) % 2, x, 2 * core + yl, (z_hi + dz) % 2, cc)
                if dz == 0:
                    @pl.when(jnp.logical_not((cc == core) & (2 * core + yl == y)))
                    def _():
                        greet(where)
                else:
                    greet(where)
    for dl, dx in GATHER:
        greet(((z_lo + dl) % 2 * 4 + (x + dx) % 4, tp))
    for dt in range(1, 16):
        greet((grp, (tp + dt) % 16))
    for lo in range(2):
        for yy in range(4):
            for hi in range(2):
                where = place(lo, chip % 4, yy, hi, core)

                @pl.when(jnp.logical_not((where[0] == grp) & (where[1] == tp)))
                def _():
                    greet(where)
    own_delta = core == y // 2
    expected = (
        1 + 8 - own_delta.astype(jnp.int32) + 7 + 15 + 16 - mine.astype(jnp.int32) - crossed.astype(jnp.int32)
    )
    own_lanes = pl.ds(pl.multiple_of(core * LOCAL, LOCAL), LOCAL)

    def act_copy(c, k):
        dl, dx = GATHER[k]
        piece = acts.at[grp, pl.ds(c * SENT_ROWS, SENT_ROWS), own_lanes]
        return pltpu.make_async_remote_copy(
            src_ref=piece, dst_ref=piece,
            send_sem=act_send.at[c * 7 + k], recv_sem=act_recv.at[c * 7 + k],
            device_id=((z_lo + dl) % 2 * 4 + (x + dx) % 4, tp), device_id_type=MESH,
        )

    def fwd_copy(c, k):
        slot = grp
        if k < 7:
            dl, dx = GATHER[k]
            slot = (z_lo + dl) % 2 * 4 + (x + 4 - dx) % 4
        piece = acts.at[slot, pl.ds(c * SENT_ROWS, SENT_ROWS), own_lanes]
        return pltpu.make_async_remote_copy(
            src_ref=piece, dst_ref=piece,
            send_sem=fwd_send.at[c * 8 + k], recv_sem=fwd_recv.at[c * 8 + k],
            device_id=partner, device_id_type=MESH,
        )

    def square_copy(k):
        return pltpu.make_async_remote_copy(
            src_ref=squares.at[tp], dst_ref=squares.at[tp],
            send_sem=square_send.at[k], recv_sem=square_recv.at[k],
            device_id=(grp, (tp + k + 1) % 16), device_id_type=MESH,
        )

    def feature_row(slab, cc):
        dz, yl = slab // 2, slab % 2
        lo, hi = (z_lo + dz) % 2, (z_hi + dz) % 2
        row = ((lo * 4 + x) * 2 + cc) * 512 + yl * 256 + hi * 128
        return pl.ds(pl.multiple_of(row, 128), 128)

    def own_copy(slab):
        return pltpu.make_async_copy(
            old_ref.at[feature_row(slab, core)],
            weight.at[pl.ds(slab * 128, 128), pl.ds(pl.multiple_of(core * LOCAL, LOCAL), LOCAL)],
            own_sem.at[slab],
        )

    def old_copy(slab):
        return pltpu.make_async_remote_copy(
            src_ref=old_ref.at[feature_row(slab, other)],
            dst_ref=weight.at[pl.ds(slab * 128, 128), pl.ds(pl.multiple_of(core * LOCAL, LOCAL), LOCAL)],
            send_sem=old_send.at[slab], recv_sem=old_recv.at[slab],
            device_id=partner, device_id_type=MESH,
        )

    def delta_copy(k):
        dy, dz = OFFSETS[k]
        first = pl.multiple_of(dz * 256 + (y % 2) * 128 + core * 64, 64)
        slot = dz * 4 + (y % 2) * 2 + core
        return pltpu.make_async_remote_copy(
            src_ref=delta.at[k], dst_ref=arrived.at[pl.ds(first, 64)],
            send_sem=delta_send.at[k], recv_sem=delta_recv.at[slot],
            device_id=place((z_lo + dz) % 2, x, (y + dy) % 4, (z_hi + dz) % 2, y // 2), device_id_type=MESH,
        )

    def delta_self():
        first = pl.multiple_of((y % 2) * 128 + core * 64, 64)
        return pltpu.make_async_copy(
            delta.at[7], arrived.at[pl.ds(first, 64)], delta_recv.at[(y % 2) * 2 + core]
        )

    small_copy(0).wait()
    scale = jnp.where(
        exps[...] == -14, 2.0**-14, jnp.where(exps[...] == -13, 2.0**-13, 2.0**-12)
    ).astype(BF16)
    block_at = lax.broadcasted_iota(jnp.int32, (64, 1024), 0)
    lane_block = lax.broadcasted_iota(jnp.int32, (64, 1024), 1) // 128
    for k in range(8):
        dy, dz = OFFSETS[k]
        column = ((y + dy) % 4) * 2 + (z_hi + dz) % 2
        pltpu.make_async_copy(codes.at[k], codes.at[k], codes_sem.at[k]).wait()
        pick = (block_at == lane_block + column * 8).astype(BF16)
        wide = jnp.dot(scale, pick, preferred_element_type=F32)
        delta[k] = (codes[k].astype(F32) * wide).astype(BF16)
    pl.semaphore_wait(barrier, expected)
    for k in range(7):
        delta_copy(k).start()

    @pl.when(own_delta)
    def _():
        delta_self().start()

    @pl.when(jnp.logical_not(own_delta))
    def _():
        delta_copy(7).start()

    for slab in range(4):
        own_copy(slab).start()
        old_copy(slab).start()

    for k in range(1, len(small)):
        small_copy(k).wait()
    group = tp // 4
    group_lanes = pl.ds(pl.multiple_of(group * STATE, STATE), STATE)
    head_of = lax.broadcasted_iota(jnp.int32, (HEADS, LOCAL), 1) // (LOCAL // HEADS)
    spread = (head_of == lax.broadcasted_iota(jnp.int32, (HEADS, LOCAL), 0)).astype(BF16)
    bias = expand_heads(jnp.broadcast_to(bias_in[...], (8, HEADS)), spread)[0:1]
    rate = expand_heads(jnp.broadcast_to(rate_in[...], (8, HEADS)), spread)[0:1]
    skip = expand_heads(jnp.broadcast_to(skip_in[...], (8, HEADS)), spread)[0:1]
    sizes, logs = [], []
    for s in range(STEPS):
        raw = lax.dot_general(dts_in[s], spread, CONTRACT_FIRST, preferred_element_type=F32) + bias
        sizes.append(jnp.maximum(raw, 0.0) + jnp.log1p(jnp.exp(-jnp.abs(raw))))
        own = sizes[s] * rate
        logs.append(own if s == 0 else logs[-1] + own)
    xs = [xs_in[s].astype(F32) for s in range(STEPS)]
    bs = [bs_in[s, :, group_lanes].astype(F32) for s in range(STEPS)]
    cs = [cs_in[s, :, group_lanes].astype(F32) for s in range(STEPS)]
    right_rows[...] = jnp.zeros(right_rows.shape, F32)
    read_rows[...] = jnp.zeros(read_rows.shape, F32)
    for s in range(STEPS):
        right_rows[0, s * ROWS:(s + 1) * ROWS, :] = bs[s]
        right_rows[0, (4 + s) * ROWS:(5 + s) * ROWS, :] = bs[s]
        read_rows[0, s * ROWS:(s + 1) * ROWS, :] = cs[s]
    right_rows[1, 8 * ROWS:11 * ROWS, :] = jnp.ones((3 * ROWS, STATE), F32)
    for s in range(STEPS):
        decay_rows[s * ROWS:(s + 1) * ROWS, :] = jnp.exp(-logs[s])
        direct = skip * xs[s]
        for u in range(s + 1):
            coef = sizes[u] if u == s else sizes[u] * jnp.exp(logs[u] - logs[s])
            term = coef * xs[u]
            direct = direct + term * jnp.sum(bs[u] * cs[s], axis=1, keepdims=True)
            if s == STEPS - 1:
                high = term.astype(BF16).astype(F32)
                put(left_rows, u * ROWS, high)
                put(left_rows, (4 + u) * ROWS, term - high)
        direct_rows[s * ROWS:(s + 1) * ROWS, :] = direct
    last = decay_rows[3 * ROWS:4 * ROWS, :]
    for at_row, part in enumerate(split3(last)):
        put(left_rows, (8 + at_row) * ROWS, part.astype(F32))
    put(left_rows, 11 * ROWS, jnp.zeros((5 * ROWS, LOCAL), F32))
    square_rows[ALL:, :] = jnp.zeros((128 - ALL, 128), F32)

    def read_one(row):
        value = held[row].reshape(LOCAL, STATE)
        high = value.astype(BF16)
        low = (value - high.astype(F32)).astype(BF16)
        both = jnp.concatenate([high, low], axis=1)
        reader = pick_rows(read_rows, row, 8).astype(BF16)
        reader = jnp.concatenate([reader, reader], axis=1)
        read = lax.dot_general(reader, both, CONTRACT_LAST, preferred_element_type=F32)
        for j in range(LOCAL // 128):
            read_state[j, pl.ds(row, 8, stride=ROWS), :] = read[:, j * 128:(j + 1) * 128]

    def update_one(row):
        left = pick_rows(left_rows, row, 16).astype(BF16)
        right = pick_rows(right_rows, row, 16).astype(BF16)
        update = lax.dot_general(left, right, CONTRACT_FIRST, preferred_element_type=F32)
        value = held[row].reshape(LOCAL, STATE)
        held[row] = (update[:, STATE:] * value + update[:, :STATE]).reshape(held.shape[1:])

    def over_rows(first, count, unroll, one):
        def some(i, carry):
            for j in range(unroll):
                one(first + i * unroll + j)
            return carry

        lax.fori_loop(0, count // unroll, some, 0)

    for c in range(CHUNKS):
        state_copy(c).wait()
        over_rows(c * CHUNK_ROWS, CHUNK_ROWS, UNROLL, read_one)
        pieces = []
        for s in range(STEPS):
            span = slice(s * ROWS + c * CHUNK_ROWS, s * ROWS + (c + 1) * CHUNK_ROWS)
            read = jnp.concatenate([read_state[j, span, :] for j in range(LOCAL // 128)], axis=1)
            z = zs_in[s].astype(F32)[c * CHUNK_ROWS:(c + 1) * CHUNK_ROWS]
            read_out = decay_rows[span, :] * read + direct_rows[span, :]
            pieces.append(read_out * (z / (1.0 + jnp.exp(-z))))
        gated = jnp.concatenate(pieces, axis=0)
        acts[grp, c * SENT_ROWS:(c + 1) * SENT_ROWS, own_lanes] = (gated * gain_in[...]).astype(BF16)
        for k in range(7):
            act_copy(c, k).start()
        fwd_copy(c, 7).start()
        total = jnp.sum(gated * gated, axis=1, keepdims=True)
        square_rows[c * SENT_ROWS:(c + 1) * SENT_ROWS, :] = jnp.broadcast_to(total, (SENT_ROWS, 128))
    squares[tp] = jnp.transpose(square_rows[...])[0:8]
    for k in range(15):
        square_copy(k).start()

    for c in range(CHUNKS):
        over_rows(c * CHUNK_ROWS, CHUNK_ROWS, UNROLL, update_one)
        for k in range(7):
            act_copy(c, k).wait_recv()
            fwd_copy(c, k).start()
    for c in range(CHUNKS):
        for k in range(8):
            fwd_copy(c, k).wait_recv()

    def part_copy(half, g):
        lo = (z_lo + half) % 2
        dest = (g, (lo * 4 + x) * 2 + core)
        slot = ((z_hi + half) % 2) * 8 + y * 2 + half
        remote = lambda: pltpu.make_async_remote_copy(
            src_ref=parts.at[half * 8 + g], dst_ref=sums.at[slot],
            send_sem=part_send.at[half * 8 + g], recv_sem=part_recv.at[slot],
            device_id=dest, device_id_type=MESH,
        )
        local = lambda: pltpu.make_async_copy(parts.at[half * 8 + g], sums.at[slot], part_recv.at[slot])
        here = (dest[0] == grp) & (dest[1] == tp)
        return remote, local, here

    for half in range(2):
        for slab in (half * 2, half * 2 + 1):
            own_copy(slab).wait()
            old_copy(slab).wait_recv()
        for slot in range(half * 4, half * 4 + 4):
            rows = arrived.at[pl.ds(slot * 64, 64)]
            pltpu.make_async_copy(rows, rows, delta_recv.at[slot]).wait()
        span = slice(half * 256, half * 256 + 256)
        fresh = (weight[span, :].astype(F32) + arrived[span, :].astype(F32)).astype(BF16)
        for quarter in range(4):
            lhs = acts[quarter * 2:quarter * 2 + 2].reshape(2 * ALL, 1024)
            got = lax.dot_general(lhs, fresh, CONTRACT_LAST, preferred_element_type=F32)
            for part in range(2):
                g = quarter * 2 + part
                parts[half * 8 + g] = got[part * ALL:(part + 1) * ALL].astype(BF16)
                remote, local, here = part_copy(half, g)

                @pl.when(here)
                def _():
                    local().start()

                @pl.when(jnp.logical_not(here))
                def _():
                    remote().start()

    for k in range(15):
        square_copy(k).wait_recv()
    for slot in range(16):
        pltpu.make_async_copy(sums.at[slot], sums.at[slot], part_recv.at[slot]).wait()

    for k in range(7):
        delta_copy(k).wait_send()
    for c in range(CHUNKS):
        for k in range(7):
            act_copy(c, k).wait_send()
        for k in range(8):
            fwd_copy(c, k).wait_send()

    @pl.when(jnp.logical_not(own_delta))
    def _():
        delta_copy(7).wait_send()
    for slab in range(4):
        old_copy(slab).wait_send()
    for k in range(15):
        square_copy(k).wait_send()
    for half in range(2):
        for g in range(8):
            remote, local, here = part_copy(half, g)

            @pl.when(jnp.logical_not(here))
            def _():
                remote().wait_send()


def finish_kernel(held, sums, squares, out_ref, final_ref, sem):
    copies = [
        pltpu.make_async_copy(held.at[pl.ds(c * 6, 6)], final_ref.at[pl.ds(c * 6, 6)], sem.at[c])
        for c in range(4)
    ]
    for copy in copies:
        copy.start()
    factors = []
    for yy in range(4):
        total = squares[4 * yy] + squares[4 * yy + 1] + squares[4 * yy + 2] + squares[4 * yy + 3]
        inverse = lax.rsqrt(total * (1.0 / GROUP_WIDTH) + 1e-05)
        factors.append(jnp.transpose(jnp.concatenate([inverse] * 16, axis=0))[0:ALL, 0:1])
    for hi in range(2):
        total = None
        for yy in range(4):
            slot = hi * 8 + yy * 2
            pair = (sums[slot].astype(F32) + sums[slot + 1].astype(F32)) * factors[yy]
            total = pair if total is None else total + pair
        for s in range(STEPS):
            rows = jnp.concatenate(
                [
                    total[c * SENT_ROWS + s * CHUNK_ROWS:c * SENT_ROWS + (s + 1) * CHUNK_ROWS]
                    for c in range(CHUNKS)
                ],
                axis=0,
            ).astype(BF16)
            for yl in range(2):
                at = yl * 256 + hi * 128
                out_ref[s, :, at:at + 128] = rows[:, yl * 128:(yl + 1) * 128]
    for copy in copies:
        copy.wait()


def local(
    old_weight, delta_codes, delta_exps, state_in, x_in, z_in, b_in, c_in, dt_in,
    dt_bias, a_rate, skip_gain, norm_gain,
):
    vmem = pl.BlockSpec(memory_space=pltpu.VMEM)
    hbm = pl.BlockSpec(memory_space=pltpu.HBM)
    dma = pltpu.SemaphoreType.DMA
    vectors = [v.reshape(1, -1) for v in (dt_bias, a_rate, skip_gain, norm_gain)]
    held, sums, squares = pl.pallas_call(
        mix_kernel,
        out_shape=(
            pltpu.VMEM(state_in.shape, F32),
            pltpu.VMEM((16, ALL, 256), BF16),
            pltpu.VMEM((16, 8, 128), F32),
        ),
        in_specs=[hbm] * 13,
        out_specs=(vmem, vmem, vmem),
        scratch_shapes=[
            pltpu.VMEM((64, 64), jnp.int32),
            pltpu.VMEM(x_in.shape, BF16),
            pltpu.VMEM(x_in.shape, BF16),
            pltpu.VMEM(b_in.shape, BF16),
            pltpu.VMEM(b_in.shape, BF16),
            pltpu.VMEM((STEPS, HEADS, ROWS), BF16),
            pltpu.VMEM((1, HEADS), F32),
            pltpu.VMEM((1, HEADS), F32),
            pltpu.VMEM((1, HEADS), F32),
            pltpu.VMEM((1, LOCAL), F32),
            pltpu.VMEM((LOCAL // 128, 16 * ROWS, 128), F32),
            pltpu.VMEM((2, 16 * ROWS, STATE), F32),
            pltpu.VMEM((1, 8 * ROWS, STATE), F32),
            pltpu.VMEM((LOCAL // 128, 8 * ROWS, 128), F32),
            pltpu.VMEM((ALL, LOCAL), F32),
            pltpu.VMEM((ALL, LOCAL), F32),
            pltpu.VMEM((128, 128), F32),
            pltpu.VMEM((8, 64, 1024), jnp.int32),
            pltpu.VMEM((8, 64, 1024), BF16),
            pltpu.VMEM((512, 1024), BF16),
            pltpu.VMEM((512, 1024), BF16),
            pltpu.VMEM((8, ALL, 1024), BF16),
            pltpu.VMEM((16, ALL, 256), BF16),
            dma((10,)), dma((CHUNKS,)), dma((8,)), dma((4,)), dma((4,)), dma((4,)), dma((8,)), dma((8,)),
            dma((7 * CHUNKS,)), dma((7 * CHUNKS,)), dma((8 * CHUNKS,)), dma((8 * CHUNKS,)),
            dma((16,)), dma((16,)), dma((15,)), dma((15,)),
        ],
        compiler_params=pltpu.CompilerParams(
            collective_id=0, has_side_effects=True, vmem_limit_bytes=36 * 1024 * 1024
        ),
        cost_estimate=pl.CostEstimate(flops=9 * 10**8, bytes_accessed=10**7, transcendentals=0),
    )(
        *[
            pltpu.with_memory_space_constraint(a, pltpu.HBM)
            for a in (
                delta_codes, delta_exps, old_weight, state_in, x_in, z_in, b_in, c_in,
                jnp.swapaxes(dt_in, 1, 2), *vectors,
            )
        ]
    )
    mixed, final_state = pl.pallas_call(
        finish_kernel,
        out_shape=(
            jax.ShapeDtypeStruct((STEPS, ROWS, LOCAL), BF16),
            jax.ShapeDtypeStruct(state_in.shape, F32),
        ),
        in_specs=[vmem] * 3,
        out_specs=(vmem, hbm),
        scratch_shapes=[dma((4,))],
        compiler_params=pltpu.CompilerParams(vmem_limit_bytes=36 * 1024 * 1024),
        cost_estimate=pl.CostEstimate(flops=10**6, bytes_accessed=7 * 10**6, transcendentals=0),
    )(held, sums, squares)
    return mixed, final_state


def solution(mesh):
    return jax.shard_map(
        local,
        mesh=mesh,
        in_specs=(
            P(None, "tp"),
            P(("grp", "tp"), None),
            P(("grp", "tp"), None),
            P("grp", "tp", None, None),
            P(None, "grp", "tp"),
            P(None, "grp", "tp"),
            P(None, "grp", None),
            P(None, "grp", None),
            P(None, "grp", "tp"),
            P("tp"),
            P("tp"),
            P("tp"),
            P("tp"),
        ),
        out_specs=(P(None, "grp", "tp"), P("grp", "tp", None, None)),
        check_vma=False,
    )
```

time: 53.2 us -> 43.5 us (0.82)
  the two profiles are of different devices: /device:TPU:40 before, /device:TPU:1 now
where the time goes in v2:
time: 43.5 us; the launch traced here: 42.8 us
  Pallas kernels  42.2 us (97%)
  between operations  0.64 us (1%)
    pallas_call x1, Pallas kernels, local(): pl.pallas_call(mix_kernel, out_shape=(pltpu.VMEM(state_in.shape, F32), pl...  38.8 us
    pallas_call x1, Pallas kernels, local(): pl.pallas_call(finish_kernel, out_shape=(jax.ShapeDtypeStruct((STEPS, ROW...  3.38 us

profile of v2, /device:TPU:1, one launch (start us, length us, event | category | flops | bytes accessed | tf_op | source)
XLA Modules:
  0.0 42.8 jit_solution(13330974213608869264)
XLA Ops:
  0.6 38.8 %shard_map.140 = (f32[24,8,64,128]{3,2,1,0:T(8,128)S(1)}, bf16[16,96,256]{2,1,0:T(8,128)(2,1)S(1)}, f32[16,8,128]{2,1,0:T(8,128)S(1)}) custom-call(s32[64,8192]{1,0:T(8,128)} %codes_ref.1, s32[64,64]{1,0:T(8,128)} %exps_ref.1, bf16[8192,512]{1,0:T(8,128)(2,1)} %old_ref.1, f32[24,8,64,128]{3,2,1,0:T(8,128)} %state_ref.1, bf16[4,24,512]{2,1,0:T(8,128)(2,1)} %x_ref.1, ...), custom_call_target="tpu_custom_call" | custom-call | flops 900000000 | bytes 10000000 | tf_op jit(solution)/shard_map/pallas_call | solution.py:439
  39.4 3.4 %shard_map.141 = (bf16[4,24,512]{2,1,0:T(8,128)(2,1)}, f32[24,8,64,128]{3,2,1,0:T(8,128)}) custom-call(f32[24,8,64,128]{3,2,1,0:T(8,128)S(1)} %get-tuple-element.5.held, bf16[16,96,256]{2,1,0:T(8,128)(2,1)S(1)} %get-tuple-element.6.sums, f32[16,8,128]{2,1,0:T(8,128)S(1)} %get-tuple-element.7.squares), custom_call_target="tpu_custom_call" | custom-call | flops 1000000 | bytes 7000000 | tf_op jit(solution)/shard_map/pallas_call | solution.py:489

commit v3 on v2

--- a/solution.py
+++ b/solution.py
@@ -51,8 +51,10 @@
 
 
 UNROLL = 4
-OFFSETS = ((2, 1), (1, 1), (3, 1), (2, 0), (1, 0), (3, 0), (0, 1), (0, 0))
-GATHER = ((0, 2), (1, 2), (0, 1), (0, 3), (1, 1), (1, 3), (1, 0))
+OFFSETS = ((2, 0), (0, 1), (1, 0), (3, 1), (3, 0), (1, 1), (2, 1), (0, 0))
+GATHER = ((0, 1), (0, 3), (0, 2), (1, 0), (1, 1), (1, 3), (1, 2))
+OWN_PLANE = (0, 1, 2, 3)
+OTHER_PLANE = (4, 5, 6)
 
 
 def mix_kernel(
@@ -61,7 +63,7 @@
     held, sums, squares,
     exps, xs_in, zs_in, bs_in, cs_in, dts_in, bias_in, rate_in, skip_in, gain_in,
     left_rows, right_rows, read_rows, read_state, decay_rows, direct_rows, square_rows,
-    codes, delta, weight, arrived, acts, parts,
+    codes, delta, weight, arrived, acts, parts, own_square, near_squares,
     small_sem, state_sem, codes_sem, own_sem, old_send, old_recv, delta_send, delta_recv,
     act_send, act_recv, fwd_send, fwd_recv, part_send, part_recv, square_send, square_recv,
 ):
@@ -117,10 +119,12 @@
                         greet(where)
                 else:
                     greet(where)
-    for dl, dx in GATHER:
+    for dl, dx in GATHER[:6]:
         greet(((z_lo + dl) % 2 * 4 + (x + dx) % 4, tp))
-    for dt in range(1, 16):
-        greet((grp, (tp + dt) % 16))
+    for cc in range(2):
+        greet(place(z_lo, x, y, 1 - z_hi, (core + cc) % 2))
+    for dy in range(1, 4):
+        greet(place(z_lo, x, (y + dy) % 4, z_hi, core))
     for lo in range(2):
         for yy in range(4):
             for hi in range(2):
@@ -131,17 +135,20 @@
                     greet(where)
     own_delta = core == y // 2
     expected = (
-        1 + 8 - own_delta.astype(jnp.int32) + 7 + 15 + 16 - mine.astype(jnp.int32) - crossed.astype(jnp.int32)
+        1 + 8 - own_delta.astype(jnp.int32) + 6 + 2 + 3 + 16 - mine.astype(jnp.int32) - crossed.astype(jnp.int32)
     )
     own_lanes = pl.ds(pl.multiple_of(core * LOCAL, LOCAL), LOCAL)
 
     def act_copy(c, k):
         dl, dx = GATHER[k]
-        piece = acts.at[grp, pl.ds(c * SENT_ROWS, SENT_ROWS), own_lanes]
+        slot, where = grp, ((z_lo + dl) % 2 * 4 + (x + dx) % 4, tp)
+        if k == 6:
+            slot, where = z_lo * 4 + (x + 2) % 4, ((z_lo + 1) % 2 * 4 + x, tp)
+        piece = acts.at[slot, pl.ds(c * SENT_ROWS, SENT_ROWS), own_lanes]
         return pltpu.make_async_remote_copy(
             src_ref=piece, dst_ref=piece,
             send_sem=act_send.at[c * 7 + k], recv_sem=act_recv.at[c * 7 + k],
-            device_id=((z_lo + dl) % 2 * 4 + (x + dx) % 4, tp), device_id_type=MESH,
+            device_id=where, device_id_type=MESH,
         )
 
     def fwd_copy(c, k):
@@ -157,10 +164,17 @@
         )
 
     def square_copy(k):
+        if k < 3:
+            other_chip, other_core = ((0, 1), (1, 0), (1, 1))[k]
+            where = place(z_lo, x, y, (z_hi + other_chip) % 2, (core + other_core) % 2)
+            source, target = own_square, near_squares.at[k]
+        else:
+            where = place(z_lo, x, (y + k - 2) % 4, z_hi, core)
+            source = target = squares.at[y]
         return pltpu.make_async_remote_copy(
-            src_ref=squares.at[tp], dst_ref=squares.at[tp],
+            src_ref=source, dst_ref=target,
             send_sem=square_send.at[k], recv_sem=square_recv.at[k],
-            device_id=(grp, (tp + k + 1) % 16), device_id_type=MESH,
+            device_id=where, device_id_type=MESH,
         )
 
     def feature_row(slab, cc):
@@ -184,20 +198,20 @@
             device_id=partner, device_id_type=MESH,
         )
 
-    def delta_copy(k):
+    def delta_copy(k, half):
         dy, dz = OFFSETS[k]
-        first = pl.multiple_of(dz * 256 + (y % 2) * 128 + core * 64, 64)
-        slot = dz * 4 + (y % 2) * 2 + core
+        slot = half * 8 + dz * 4 + (y % 2) * 2 + core
         return pltpu.make_async_remote_copy(
-            src_ref=delta.at[k], dst_ref=arrived.at[pl.ds(first, 64)],
-            send_sem=delta_send.at[k], recv_sem=delta_recv.at[slot],
+            src_ref=delta.at[k, pl.ds(half * 32, 32)], dst_ref=arrived.at[pl.ds(pl.multiple_of(slot * 32, 32), 32)],
+            send_sem=delta_send.at[half * 8 + k], recv_sem=delta_recv.at[slot],
             device_id=place((z_lo + dz) % 2, x, (y + dy) % 4, (z_hi + dz) % 2, y // 2), device_id_type=MESH,
         )
 
-    def delta_self():
-        first = pl.multiple_of((y % 2) * 128 + core * 64, 64)
+    def delta_self(half):
+        slot = half * 8 + (y % 2) * 2 + core
         return pltpu.make_async_copy(
-            delta.at[7], arrived.at[pl.ds(first, 64)], delta_recv.at[(y % 2) * 2 + core]
+            delta.at[7, pl.ds(half * 32, 32)], arrived.at[pl.ds(pl.multiple_of(slot * 32, 32), 32)],
+            delta_recv.at[slot],
         )
 
     small_copy(0).wait()
@@ -213,18 +227,24 @@
         pick = (block_at == lane_block + column * 8).astype(BF16)
         wide = jnp.dot(scale, pick, preferred_element_type=F32)
         delta[k] = (codes[k].astype(F32) * wide).astype(BF16)
-    pl.semaphore_wait(barrier, expected)
-    for k in range(7):
-        delta_copy(k).start()
+        if k == 1:
+            pl.semaphore_wait(barrier, expected)
+            delta_copy(0, 0).start()
+        if 1 <= k < 7:
+            delta_copy(k, 0).start()
 
     @pl.when(own_delta)
     def _():
-        delta_self().start()
+        for half in range(2):
+            delta_self(half).start()
 
     @pl.when(jnp.logical_not(own_delta))
     def _():
-        delta_copy(7).start()
-
+        for half in range(2):
+            delta_copy(7, half).start()
+
+    for k in range(7):
+        delta_copy(k, 1).start()
     for slab in range(4):
         own_copy(slab).start()
         old_copy(slab).start()
@@ -310,69 +330,95 @@
             pieces.append(read_out * (z / (1.0 + jnp.exp(-z))))
         gated = jnp.concatenate(pieces, axis=0)
         acts[grp, c * SENT_ROWS:(c + 1) * SENT_ROWS, own_lanes] = (gated * gain_in[...]).astype(BF16)
-        for k in range(7):
+        for k in OWN_PLANE:
             act_copy(c, k).start()
         fwd_copy(c, 7).start()
         total = jnp.sum(gated * gated, axis=1, keepdims=True)
         square_rows[c * SENT_ROWS:(c + 1) * SENT_ROWS, :] = jnp.broadcast_to(total, (SENT_ROWS, 128))
-    squares[tp] = jnp.transpose(square_rows[...])[0:8]
-    for k in range(15):
+    for c in range(CHUNKS):
+        for k in (4, 5):
+            act_copy(c, k).start()
+    own_square[...] = jnp.transpose(square_rows[...])[0:8]
+    for k in range(3):
         square_copy(k).start()
 
     for c in range(CHUNKS):
         over_rows(c * CHUNK_ROWS, CHUNK_ROWS, UNROLL, update_one)
-        for k in range(7):
+        for k in OWN_PLANE:
             act_copy(c, k).wait_recv()
             fwd_copy(c, k).start()
-    for c in range(CHUNKS):
-        for k in range(8):
-            fwd_copy(c, k).wait_recv()
-
-    def part_copy(half, g):
-        lo = (z_lo + half) % 2
-        dest = (g, (lo * 4 + x) * 2 + core)
-        slot = ((z_hi + half) % 2) * 8 + y * 2 + half
+            if k == 2:
+                act_copy(c, 6).start()
+    for k in range(3):
+        square_copy(k).wait_recv()
+    squares[y] = own_square[...] + near_squares[0] + near_squares[1] + near_squares[2]
+    for k in range(3, 6):
+        square_copy(k).start()
+
+    def part_copy(half, plane, dz, i):
+        g = (z_lo + plane) % 2 * 4 + i
+        dest = (g, ((z_lo + dz) % 2 * 4 + x) * 2 + core)
+        at = ((half * 2 + plane) * 2 + dz) * 4 + i
+        slot = (half * 2 + (z_hi + dz) % 2) * 8 + y * 2 + dz
         remote = lambda: pltpu.make_async_remote_copy(
-            src_ref=parts.at[half * 8 + g], dst_ref=sums.at[slot],
-            send_sem=part_send.at[half * 8 + g], recv_sem=part_recv.at[slot],
+            src_ref=parts.at[at], dst_ref=sums.at[slot],
+            send_sem=part_send.at[at], recv_sem=part_recv.at[slot],
             device_id=dest, device_id_type=MESH,
         )
-        local = lambda: pltpu.make_async_copy(parts.at[half * 8 + g], sums.at[slot], part_recv.at[slot])
+        local = lambda: pltpu.make_async_copy(parts.at[at], sums.at[slot], part_recv.at[slot])
         here = (dest[0] == grp) & (dest[1] == tp)
-        return remote, local, here
-
+        return at, remote, local, here
+
+    for slab in range(4):
+        own_copy(slab).wait()
+        old_copy(slab).wait_recv()
     for half in range(2):
-        for slab in (half * 2, half * 2 + 1):
-            own_copy(slab).wait()
-            old_copy(slab).wait_recv()
-        for slot in range(half * 4, half * 4 + 4):
-            rows = arrived.at[pl.ds(slot * 64, 64)]
+        for slot in range(half * 8, half * 8 + 8):
+            rows = arrived.at[pl.ds(slot * 32, 32)]
             pltpu.make_async_copy(rows, rows, delta_recv.at[slot]).wait()
-        span = slice(half * 256, half * 256 + 256)
-        fresh = (weight[span, :].astype(F32) + arrived[span, :].astype(F32)).astype(BF16)
-        for quarter in range(4):
-            lhs = acts[quarter * 2:quarter * 2 + 2].reshape(2 * ALL, 1024)
-            got = lax.dot_general(lhs, fresh, CONTRACT_LAST, preferred_element_type=F32)
-            for part in range(2):
-                g = quarter * 2 + part
-                parts[half * 8 + g] = got[part * ALL:(part + 1) * ALL].astype(BF16)
-                remote, local, here = part_copy(half, g)
-
-                @pl.when(here)
-                def _():
-                    local().start()
-
-                @pl.when(jnp.logical_not(here))
-                def _():
-                    remote().start()
-
-    for k in range(15):
+        fresh = []
+        for q in range(8):
+            first = q * 64 + half * 32
+            coming = half * 256 + q * 32
+            fresh.append(
+                (weight[first:first + 32, :].astype(F32) + arrived[coming:coming + 32, :].astype(F32)).astype(BF16)
+            )
+        fresh = jnp.concatenate(fresh, axis=0)
+        for plane in range(2):
+            if half == 0:
+                if plane == 1:
+                    for c in range(CHUNKS):
+                        for k in OTHER_PLANE:
+                            act_copy(c, k).wait_recv()
+                            fwd_copy(c, k).start()
+                for c in range(CHUNKS):
+                    for k in ((7, 0, 1, 2), (3, 4, 5, 6))[plane]:
+                        fwd_copy(c, k).wait_recv()
+            for pair in range(2):
+                start = (z_lo + plane) % 2 * 4 + pair * 2
+                lhs = acts[pl.ds(start, 2)].reshape(2 * ALL, 1024)
+                got = lax.dot_general(lhs, fresh, CONTRACT_LAST, preferred_element_type=F32)
+                for part in range(2):
+                    for dz in range(2):
+                        at, remote, local, here = part_copy(half, plane, dz, pair * 2 + part)
+                        parts[at] = got[part * ALL:(part + 1) * ALL, dz * 128:dz * 128 + 128].astype(BF16)
+
+                        @pl.when(here)
+                        def _():
+                            local().start()
+
+                        @pl.when(jnp.logical_not(here))
+                        def _():
+                            remote().start()
+
+    for k in range(3, 6):
         square_copy(k).wait_recv()
-    for slot in range(16):
+    for slot in range(32):
         pltpu.make_async_copy(sums.at[slot], sums.at[slot], part_recv.at[slot]).wait()
 
     for k in range(7):
-        delta_copy(k).wait_send()
+        for half in range(2):
+            delta_copy(k, half).wait_send()
     for c in range(CHUNKS):
         for k in range(7):
             act_copy(c, k).wait_send()
@@ -381,18 +427,21 @@
 
     @pl.when(jnp.logical_not(own_delta))
     def _():
-        delta_copy(7).wait_send()
+        for half in range(2):
+            delta_copy(7, half).wait_send()
     for slab in range(4):
         old_copy(slab).wait_send()
-    for k in range(15):
+    for k in range(6):
         square_copy(k).wait_send()
     for half in range(2):
-        for g in range(8):
-            remote, local, here = part_copy(half, g)
-
-            @pl.when(jnp.logical_not(here))
-            def _():
-                remote().wait_send()
+        for plane in range(2):
+            for dz in range(2):
+                for i in range(4):
+                    _, remote, _, here = part_copy(half, plane, dz, i)
+
+                    @pl.when(jnp.logical_not(here))
+                    def _():
+                        remote().wait_send()
 
 
 def finish_kernel(held, sums, squares, out_ref, final_ref, sem):
@@ -404,15 +453,21 @@
         copy.start()
     factors = []
     for yy in range(4):
-        total = squares[4 * yy] + squares[4 * yy + 1] + squares[4 * yy + 2] + squares[4 * yy + 3]
-        inverse = lax.rsqrt(total * (1.0 / GROUP_WIDTH) + 1e-05)
+        inverse = lax.rsqrt(squares[yy] * (1.0 / GROUP_WIDTH) + 1e-05)
         factors.append(jnp.transpose(jnp.concatenate([inverse] * 16, axis=0))[0:ALL, 0:1])
+    lane = lax.broadcasted_iota(jnp.int32, (256, 256), 1)
+    source = (lane // 32) % 2 * 128 + lane // 128 * 64 + (lane // 64) % 2 * 32 + lane % 32
+    order = (lax.broadcasted_iota(jnp.int32, (256, 256), 0) == source).astype(BF16)
     for hi in range(2):
-        total = None
-        for yy in range(4):
-            slot = hi * 8 + yy * 2
-            pair = (sums[slot].astype(F32) + sums[slot + 1].astype(F32)) * factors[yy]
-            total = pair if total is None else total + pair
+        totals = []
+        for half in range(2):
+            total = None
+            for yy in range(4):
+                slot = (half * 2 + hi) * 8 + yy * 2
+                pair = (sums[slot].astype(F32) + sums[slot + 1].astype(F32)) * factors[yy]
+                total = pair if total is None else total + pair
+            totals.append(total.astype(BF16))
+        total = jnp.dot(jnp.concatenate(totals, axis=1), order, preferred_element_type=F32)
         for s in range(STEPS):
             rows = jnp.concatenate(
                 [
@@ -440,8 +495,8 @@
         mix_kernel,
         out_shape=(
             pltpu.VMEM(state_in.shape, F32),
-            pltpu.VMEM((16, ALL, 256), BF16),
-            pltpu.VMEM((16, 8, 128), F32),
+            pltpu.VMEM((32, ALL, 128), BF16),
+            pltpu.VMEM((4, 8, 128), F32),
         ),
         in_specs=[hbm] * 13,
         out_specs=(vmem, vmem, vmem),
@@ -468,10 +523,12 @@
             pltpu.VMEM((512, 1024), BF16),
             pltpu.VMEM((512, 1024), BF16),
             pltpu.VMEM((8, ALL, 1024), BF16),
-            pltpu.VMEM((16, ALL, 256), BF16),
-            dma((10,)), dma((CHUNKS,)), dma((8,)), dma((4,)), dma((4,)), dma((4,)), dma((8,)), dma((8,)),
+            pltpu.VMEM((32, ALL, 128), BF16),
+            pltpu.VMEM((8, 128), F32),
+            pltpu.VMEM((3, 8, 128), F32),
+            dma((10,)), dma((CHUNKS,)), dma((8,)), dma((4,)), dma((4,)), dma((4,)), dma((16,)), dma((16,)),
             dma((7 * CHUNKS,)), dma((7 * CHUNKS,)), dma((8 * CHUNKS,)), dma((8 * CHUNKS,)),
-            dma((16,)), dma((16,)), dma((15,)), dma((15,)),
+            dma((32,)), dma((32,)), dma((6,)), dma((6,)),
         ],
         compiler_params=pltpu.CompilerParams(
             collective_id=0, has_side_effects=True, vmem_limit_bytes=36 * 1024 * 1024

time: 43.5 us -> 42 us (0.966); the launches traced: 42.8 us -> 41.9 us
  Pallas kernels: 42.2 us -> 41.3 us
    pallas_call x1, Pallas kernels: 38.8 us -> 37.9 us  [local(): pl.pallas_call(mix_kernel, out_shape=(pltpu.VMEM(state_in.shape, F32), pl...]
where the time goes in v3:
time: 42 us; the launch traced here: 41.9 us
  Pallas kernels  41.3 us (98%)
  between operations  0.64 us (2%)
    pallas_call x1, Pallas kernels, local(): pl.pallas_call(mix_kernel, out_shape=(pltpu.VMEM(state_in.shape, F32), pl...  37.9 us
    pallas_call x1, Pallas kernels, local(): pl.pallas_call(finish_kernel, out_shape=(jax.ShapeDtypeStruct((STEPS, ROW...  3.37 us

profile of v3, /device:TPU:1, one launch (start us, length us, event | category | flops | bytes accessed | tf_op | source)
XLA Modules:
  0.0 41.9 jit_solution(5031477006673919412)
XLA Ops:
  0.6 37.9 %shard_map.140 = (f32[24,8,64,128]{3,2,1,0:T(8,128)S(1)}, bf16[32,96,128]{2,1,0:T(8,128)(2,1)S(1)}, f32[4,8,128]{2,1,0:T(8,128)S(1)}) custom-call(s32[64,8192]{1,0:T(8,128)} %codes_ref.1, s32[64,64]{1,0:T(8,128)} %exps_ref.1, bf16[8192,512]{1,0:T(8,128)(2,1)} %old_ref.1, f32[24,8,64,128]{3,2,1,0:T(8,128)} %state_ref.1, bf16[4,24,512]{2,1,0:T(8,128)(2,1)} %x_ref.1, ...), custom_call_target="tpu_custom_call" | custom-call | flops 900000000 | bytes 10000000 | tf_op jit(solution)/shard_map/pallas_call | solution.py:494
  38.5 3.4 %shard_map.141 = (bf16[4,24,512]{2,1,0:T(8,128)(2,1)}, f32[24,8,64,128]{3,2,1,0:T(8,128)}) custom-call(f32[24,8,64,128]{3,2,1,0:T(8,128)S(1)} %get-tuple-element.5.held, bf16[32,96,128]{2,1,0:T(8,128)(2,1)S(1)} %get-tuple-element.6.sums, f32[4,8,128]{2,1,0:T(8,128)S(1)} %get-tuple-element.7.squares), custom_call_target="tpu_custom_call" | custom-call | flops 1000000 | bytes 7000000 | tf_op jit(solution)/shard_map/pallas_call | solution.py:546

commit v4 on v3

--- a/solution.py
+++ b/solution.py
@@ -100,8 +100,6 @@
 
     for k in range(len(small)):
         small_copy(k).start()
-    for c in range(CHUNKS):
-        state_copy(c).start()
 
     barrier = pltpu.get_barrier_semaphore()
 
@@ -224,30 +222,12 @@
         dy, dz = OFFSETS[k]
         column = ((y + dy) % 4) * 2 + (z_hi + dz) % 2
         pltpu.make_async_copy(codes.at[k], codes.at[k], codes_sem.at[k]).wait()
+        if k == 3:
+            for c in range(CHUNKS):
+                state_copy(c).start()
         pick = (block_at == lane_block + column * 8).astype(BF16)
         wide = jnp.dot(scale, pick, preferred_element_type=F32)
         delta[k] = (codes[k].astype(F32) * wide).astype(BF16)
-        if k == 1:
-            pl.semaphore_wait(barrier, expected)
-            delta_copy(0, 0).start()
-        if 1 <= k < 7:
-            delta_copy(k, 0).start()
-
-    @pl.when(own_delta)
-    def _():
-        for half in range(2):
-            delta_self(half).start()
-
-    @pl.when(jnp.logical_not(own_delta))
-    def _():
-        for half in range(2):
-            delta_copy(7, half).start()
-
-    for k in range(7):
-        delta_copy(k, 1).start()
-    for slab in range(4):
-        own_copy(slab).start()
-        old_copy(slab).start()
 
     for k in range(1, len(small)):
         small_copy(k).wait()
@@ -292,6 +272,26 @@
     put(left_rows, 11 * ROWS, jnp.zeros((5 * ROWS, LOCAL), F32))
     square_rows[ALL:, :] = jnp.zeros((128 - ALL, 128), F32)
 
+    pl.semaphore_wait(barrier, expected)
+    for k in range(7):
+        delta_copy(k, 0).start()
+
+    @pl.when(own_delta)
+    def _():
+        for half in range(2):
+            delta_self(half).start()
+
+    @pl.when(jnp.logical_not(own_delta))
+    def _():
+        for half in range(2):
+            delta_copy(7, half).start()
+
+    for k in range(7):
+        delta_copy(k, 1).start()
+    for slab in range(4):
+        own_copy(slab).start()
+        old_copy(slab).start()
+
     def read_one(row):
         value = held[row].reshape(LOCAL, STATE)
         high = value.astype(BF16)
@@ -349,11 +349,6 @@
             fwd_copy(c, k).start()
             if k == 2:
                 act_copy(c, 6).start()
-    for k in range(3):
-        square_copy(k).wait_recv()
-    squares[y] = own_square[...] + near_squares[0] + near_squares[1] + near_squares[2]
-    for k in range(3, 6):
-        square_copy(k).start()
 
     def part_copy(half, plane, dz, i):
         g = (z_lo + plane) % 2 * 4 + i
@@ -394,11 +389,11 @@
                 for c in range(CHUNKS):
                     for k in ((7, 0, 1, 2), (3, 4, 5, 6))[plane]:
                         fwd_copy(c, k).wait_recv()
-            for pair in range(2):
-                start = (z_lo + plane) % 2 * 4 + pair * 2
-                lhs = acts[pl.ds(start, 2)].reshape(2 * ALL, 1024)
+            for pair in range(1):
+                start = (z_lo + plane) % 2 * 4
+                lhs = acts[pl.ds(start, 4)].reshape(4 * ALL, 1024)
                 got = lax.dot_general(lhs, fresh, CONTRACT_LAST, preferred_element_type=F32)
-                for part in range(2):
+                for part in range(4):
                     for dz in range(2):
                         at, remote, local, here = part_copy(half, plane, dz, pair * 2 + part)
                         parts[at] = got[part * ALL:(part + 1) * ALL, dz * 128:dz * 128 + 128].astype(BF16)
@@ -411,6 +406,11 @@
                         def _():
                             remote().start()
 
+    for k in range(3):
+        square_copy(k).wait_recv()
+    squares[y] = own_square[...] + near_squares[0] + near_squares[1] + near_squares[2]
+    for k in range(3, 6):
+        square_copy(k).start()
     for k in range(3, 6):
         square_copy(k).wait_recv()
     for slot in range(32):

time: 42 us -> 40.3 us (0.960)
  Pallas kernels: 41.3 us -> 39.6 us
    pallas_call x1, Pallas kernels: 37.9 us -> 36.2 us  [local(): pl.pallas_call(mix_kernel, out_shape=(pltpu.VMEM(state_in.shape, F32), pl...]
where the time goes in v4:
time: 40.3 us; the launch traced here: 40.2 us
  Pallas kernels  39.6 us (98%)
  between operations  0.64 us (2%)
    pallas_call x1, Pallas kernels, local(): pl.pallas_call(mix_kernel, out_shape=(pltpu.VMEM(state_in.shape, F32), pl...  36.2 us
    pallas_call x1, Pallas kernels, local(): pl.pallas_call(finish_kernel, out_shape=(jax.ShapeDtypeStruct((STEPS, ROW...  3.37 us

profile of v4, /device:TPU:1, one launch (start us, length us, event | category | flops | bytes accessed | tf_op | source)
XLA Modules:
  0.0 40.2 jit_solution(10191488483108267506)
XLA Ops:
  0.6 36.2 %shard_map.140 = (f32[24,8,64,128]{3,2,1,0:T(8,128)S(1)}, bf16[32,96,128]{2,1,0:T(8,128)(2,1)S(1)}, f32[4,8,128]{2,1,0:T(8,128)S(1)}) custom-call(s32[64,8192]{1,0:T(8,128)} %codes_ref.1, s32[64,64]{1,0:T(8,128)} %exps_ref.1, bf16[8192,512]{1,0:T(8,128)(2,1)} %old_ref.1, f32[24,8,64,128]{3,2,1,0:T(8,128)} %state_ref.1, bf16[4,24,512]{2,1,0:T(8,128)(2,1)} %x_ref.1, ...), custom_call_target="tpu_custom_call" | custom-call | flops 900000000 | bytes 10000000 | tf_op jit(solution)/shard_map/pallas_call | solution.py:494
  36.8 3.4 %shard_map.141 = (bf16[4,24,512]{2,1,0:T(8,128)(2,1)}, f32[24,8,64,128]{3,2,1,0:T(8,128)}) custom-call(f32[24,8,64,128]{3,2,1,0:T(8,128)S(1)} %get-tuple-element.5.held, bf16[32,96,128]{2,1,0:T(8,128)(2,1)S(1)} %get-tuple-element.6.sums, f32[4,8,128]{2,1,0:T(8,128)S(1)} %get-tuple-element.7.squares), custom_call_target="tpu_custom_call" | custom-call | flops 1000000 | bytes 7000000 | tf_op jit(solution)/shard_map/pallas_call | solution.py:546

commit v5 on v4

--- a/solution.py
+++ b/solution.py
@@ -51,6 +51,7 @@
 
 
 UNROLL = 4
+PART_ORDER = ((1, 0), (1, 1), (3, 0), (3, 1), (2, 0), (2, 1), (0, 0), (0, 1))
 OFFSETS = ((2, 0), (0, 1), (1, 0), (3, 1), (3, 0), (1, 1), (2, 1), (0, 0))
 GATHER = ((0, 1), (0, 3), (0, 2), (1, 0), (1, 1), (1, 3), (1, 2))
 OWN_PLANE = (0, 1, 2, 3)
@@ -145,7 +146,7 @@
         piece = acts.at[slot, pl.ds(c * SENT_ROWS, SENT_ROWS), own_lanes]
         return pltpu.make_async_remote_copy(
             src_ref=piece, dst_ref=piece,
-            send_sem=act_send.at[c * 7 + k], recv_sem=act_recv.at[c * 7 + k],
+            send_sem=act_send, recv_sem=act_recv.at[c * 7 + k],
             device_id=where, device_id_type=MESH,
         )
 
@@ -157,7 +158,7 @@
         piece = acts.at[slot, pl.ds(c * SENT_ROWS, SENT_ROWS), own_lanes]
         return pltpu.make_async_remote_copy(
             src_ref=piece, dst_ref=piece,
-            send_sem=fwd_send.at[c * 8 + k], recv_sem=fwd_recv.at[c * 8 + k],
+            send_sem=fwd_send, recv_sem=fwd_recv.at[0 if k in (7, 0, 1, 2) else 1],
             device_id=partner, device_id_type=MESH,
         )
 
@@ -201,7 +202,7 @@
         slot = half * 8 + dz * 4 + (y % 2) * 2 + core
         return pltpu.make_async_remote_copy(
             src_ref=delta.at[k, pl.ds(half * 32, 32)], dst_ref=arrived.at[pl.ds(pl.multiple_of(slot * 32, 32), 32)],
-            send_sem=delta_send.at[half * 8 + k], recv_sem=delta_recv.at[slot],
+            send_sem=delta_send.at[0 if k < 7 else 1 + half], recv_sem=delta_recv.at[half],
             device_id=place((z_lo + dz) % 2, x, (y + dy) % 4, (z_hi + dz) % 2, y // 2), device_id_type=MESH,
         )
 
@@ -209,7 +210,7 @@
         slot = half * 8 + (y % 2) * 2 + core
         return pltpu.make_async_copy(
             delta.at[7, pl.ds(half * 32, 32)], arrived.at[pl.ds(pl.multiple_of(slot * 32, 32), 32)],
-            delta_recv.at[slot],
+            delta_recv.at[half],
         )
 
     small_copy(0).wait()
@@ -276,22 +277,6 @@
     for k in range(7):
         delta_copy(k, 0).start()
 
-    @pl.when(own_delta)
-    def _():
-        for half in range(2):
-            delta_self(half).start()
-
-    @pl.when(jnp.logical_not(own_delta))
-    def _():
-        for half in range(2):
-            delta_copy(7, half).start()
-
-    for k in range(7):
-        delta_copy(k, 1).start()
-    for slab in range(4):
-        own_copy(slab).start()
-        old_copy(slab).start()
-
     def read_one(row):
         value = held[row].reshape(LOCAL, STATE)
         high = value.astype(BF16)
@@ -335,6 +320,22 @@
         fwd_copy(c, 7).start()
         total = jnp.sum(gated * gated, axis=1, keepdims=True)
         square_rows[c * SENT_ROWS:(c + 1) * SENT_ROWS, :] = jnp.broadcast_to(total, (SENT_ROWS, 128))
+    @pl.when(own_delta)
+    def _():
+        for half in range(2):
+            delta_self(half).start()
+
+    @pl.when(jnp.logical_not(own_delta))
+    def _():
+        for half in range(2):
+            delta_copy(7, half).start()
+
+    for k in range(7):
+        delta_copy(k, 1).start()
+    for slab in range(4):
+        own_copy(slab).start()
+        old_copy(slab).start()
+
     for c in range(CHUNKS):
         for k in (4, 5):
             act_copy(c, k).start()
@@ -357,10 +358,10 @@
         slot = (half * 2 + (z_hi + dz) % 2) * 8 + y * 2 + dz
         remote = lambda: pltpu.make_async_remote_copy(
             src_ref=parts.at[at], dst_ref=sums.at[slot],
-            send_sem=part_send.at[at], recv_sem=part_recv.at[slot],
+            send_sem=part_send.at[at], recv_sem=part_recv,
             device_id=dest, device_id_type=MESH,
         )
-        local = lambda: pltpu.make_async_copy(parts.at[at], sums.at[slot], part_recv.at[slot])
+        local = lambda: pltpu.make_async_copy(parts.at[at], sums.at[slot], part_recv)
         here = (dest[0] == grp) & (dest[1] == tp)
         return at, remote, local, here
 
@@ -368,9 +369,8 @@
         own_copy(slab).wait()
         old_copy(slab).wait_recv()
     for half in range(2):
-        for slot in range(half * 8, half * 8 + 8):
-            rows = arrived.at[pl.ds(slot * 32, 32)]
-            pltpu.make_async_copy(rows, rows, delta_recv.at[slot]).wait()
+        rows = arrived.at[pl.ds(half * 256, 256)]
+        pltpu.make_async_copy(rows, rows, delta_recv.at[half]).wait()
         fresh = []
         for q in range(8):
             first = q * 64 + half * 32
@@ -386,25 +386,27 @@
                         for k in OTHER_PLANE:
                             act_copy(c, k).wait_recv()
                             fwd_copy(c, k).start()
-                for c in range(CHUNKS):
-                    for k in ((7, 0, 1, 2), (3, 4, 5, 6))[plane]:
-                        fwd_copy(c, k).wait_recv()
+                other_lanes = pl.ds(pl.multiple_of(other * LOCAL, LOCAL), LOCAL)
+                rows = acts.at[pl.ds((z_lo + plane) % 2 * 4, 4), :, other_lanes]
+                pltpu.make_async_copy(rows, rows, fwd_recv.at[plane]).wait()
             for pair in range(1):
                 start = (z_lo + plane) % 2 * 4
                 lhs = acts[pl.ds(start, 4)].reshape(4 * ALL, 1024)
                 got = lax.dot_general(lhs, fresh, CONTRACT_LAST, preferred_element_type=F32)
                 for part in range(4):
                     for dz in range(2):
-                        at, remote, local, here = part_copy(half, plane, dz, pair * 2 + part)
+                        at = ((half * 2 + plane) * 2 + dz) * 4 + part
                         parts[at] = got[part * ALL:(part + 1) * ALL, dz * 128:dz * 128 + 128].astype(BF16)
-
-                        @pl.when(here)
-                        def _():
-                            local().start()
-
-                        @pl.when(jnp.logical_not(here))
-                        def _():
-                            remote().start()
+                for dx, dz in PART_ORDER:
+                    _, remote, local, here = part_copy(half, plane, dz, (x + dx) % 4)
+
+                    @pl.when(here)
+                    def _():
+                        local().start()
+
+                    @pl.when(jnp.logical_not(here))
+                    def _():
+                        remote().start()
 
     for k in range(3):
         square_copy(k).wait_recv()
@@ -413,17 +415,10 @@
         square_copy(k).start()
     for k in range(3, 6):
         square_copy(k).wait_recv()
-    for slot in range(32):
-        pltpu.make_async_copy(sums.at[slot], sums.at[slot], part_recv.at[slot]).wait()
-
-    for k in range(7):
-        for half in range(2):
-            delta_copy(k, half).wait_send()
-    for c in range(CHUNKS):
-        for k in range(7):
-            act_copy(c, k).wait_send()
-        for k in range(8):
-            fwd_copy(c, k).wait_send()
+    pltpu.make_async_copy(delta.at[pl.ds(0, 7)], delta.at[pl.ds(0, 7)], delta_send.at[0]).wait()
+    for count, sem in ((7, act_send), (8, fwd_send)):
+        rows = acts.at[pl.ds(0, count), :, own_lanes]
+        pltpu.make_async_copy(rows, rows, sem).wait()
 
     @pl.when(jnp.logical_not(own_delta))
     def _():
@@ -442,6 +437,7 @@
                     @pl.when(jnp.logical_not(here))
                     def _():
                         remote().wait_send()
+    pltpu.make_async_copy(sums, sums, part_recv).wait()
 
 
 def finish_kernel(held, sums, squares, out_ref, final_ref, sem):
@@ -526,9 +522,9 @@
             pltpu.VMEM((32, ALL, 128), BF16),
             pltpu.VMEM((8, 128), F32),
             pltpu.VMEM((3, 8, 128), F32),
-            dma((10,)), dma((CHUNKS,)), dma((8,)), dma((4,)), dma((4,)), dma((4,)), dma((16,)), dma((16,)),
-            dma((7 * CHUNKS,)), dma((7 * CHUNKS,)), dma((8 * CHUNKS,)), dma((8 * CHUNKS,)),
-            dma((32,)), dma((32,)), dma((6,)), dma((6,)),
+            dma((10,)), dma((CHUNKS,)), dma((8,)), dma((4,)), dma((4,)), dma((4,)), dma((3,)), dma((2,)),
+            dma, dma((7 * CHUNKS,)), dma, dma((2,)),
+            dma((32,)), dma, dma((6,)), dma((6,)),
         ],
         compiler_params=pltpu.CompilerParams(
             collective_id=0, has_side_effects=True, vmem_limit_bytes=36 * 1024 * 1024

time: 40.3 us -> 38.5 us (0.955)
  Pallas kernels: 39.6 us -> 37.7 us
    pallas_call x1, Pallas kernels: 36.2 us -> 34.3 us  [local(): pl.pallas_call(mix_kernel, out_shape=(pltpu.VMEM(state_in.shape, F32), pl...]
where the time goes in v5:
time: 38.5 us; the launch traced here: 38.4 us
  Pallas kernels  37.7 us (98%)
  between operations  0.64 us (2%)
    pallas_call x1, Pallas kernels, local(): pl.pallas_call(mix_kernel, out_shape=(pltpu.VMEM(state_in.shape, F32), pl...  34.3 us
    pallas_call x1, Pallas kernels, local(): pl.pallas_call(finish_kernel, out_shape=(jax.ShapeDtypeStruct((STEPS, ROW...  3.37 us

profile of v5, /device:TPU:1, one launch (start us, length us, event | category | flops | bytes accessed | tf_op | source)
XLA Modules:
  0.0 38.4 jit_solution(9019737965353586991)
XLA Ops:
  0.6 34.3 %shard_map.140 = (f32[24,8,64,128]{3,2,1,0:T(8,128)S(1)}, bf16[32,96,128]{2,1,0:T(8,128)(2,1)S(1)}, f32[4,8,128]{2,1,0:T(8,128)S(1)}) custom-call(s32[64,8192]{1,0:T(8,128)} %codes_ref.1, s32[64,64]{1,0:T(8,128)} %exps_ref.1, bf16[8192,512]{1,0:T(8,128)(2,1)} %old_ref.1, f32[24,8,64,128]{3,2,1,0:T(8,128)} %state_ref.1, bf16[4,24,512]{2,1,0:T(8,128)(2,1)} %x_ref.1, ...), custom_call_target="tpu_custom_call" | custom-call | flops 900000000 | bytes 10000000 | tf_op jit(solution)/shard_map/pallas_call | solution.py:490
  35.0 3.4 %shard_map.141 = (bf16[4,24,512]{2,1,0:T(8,128)(2,1)}, f32[24,8,64,128]{3,2,1,0:T(8,128)}) custom-call(f32[24,8,64,128]{3,2,1,0:T(8,128)S(1)} %get-tuple-element.5.held, bf16[32,96,128]{2,1,0:T(8,128)(2,1)S(1)} %get-tuple-element.6.sums, f32[4,8,128]{2,1,0:T(8,128)S(1)} %get-tuple-element.7.squares), custom_call_target="tpu_custom_call" | custom-call | flops 1000000 | bytes 7000000 | tf_op jit(solution)/shard_map/pallas_call | solution.py:542

commit v6 on v5

--- a/solution.py
+++ b/solution.py
@@ -186,14 +186,14 @@
         return pltpu.make_async_copy(
             old_ref.at[feature_row(slab, core)],
             weight.at[pl.ds(slab * 128, 128), pl.ds(pl.multiple_of(core * LOCAL, LOCAL), LOCAL)],
-            own_sem.at[slab],
+            own_sem,
         )
 
     def old_copy(slab):
         return pltpu.make_async_remote_copy(
             src_ref=old_ref.at[feature_row(slab, other)],
             dst_ref=weight.at[pl.ds(slab * 128, 128), pl.ds(pl.multiple_of(core * LOCAL, LOCAL), LOCAL)],
-            send_sem=old_send.at[slab], recv_sem=old_recv.at[slab],
+            send_sem=old_send, recv_sem=old_recv,
             device_id=partner, device_id_type=MESH,
         )
 
@@ -315,7 +315,7 @@
             pieces.append(read_out * (z / (1.0 + jnp.exp(-z))))
         gated = jnp.concatenate(pieces, axis=0)
         acts[grp, c * SENT_ROWS:(c + 1) * SENT_ROWS, own_lanes] = (gated * gain_in[...]).astype(BF16)
-        for k in OWN_PLANE:
+        for k in range(6):
             act_copy(c, k).start()
         fwd_copy(c, 7).start()
         total = jnp.sum(gated * gated, axis=1, keepdims=True)
@@ -336,38 +336,37 @@
         own_copy(slab).start()
         old_copy(slab).start()
 
-    for c in range(CHUNKS):
-        for k in (4, 5):
-            act_copy(c, k).start()
     own_square[...] = jnp.transpose(square_rows[...])[0:8]
     for k in range(3):
         square_copy(k).start()
 
+    over_rows(0, ROWS, UNROLL, update_one)
     for c in range(CHUNKS):
-        over_rows(c * CHUNK_ROWS, CHUNK_ROWS, UNROLL, update_one)
         for k in OWN_PLANE:
             act_copy(c, k).wait_recv()
             fwd_copy(c, k).start()
             if k == 2:
                 act_copy(c, 6).start()
 
-    def part_copy(half, plane, dz, i):
+    def part_copy(half, plane, dz, dx):
+        i = (x + dx) % 4
         g = (z_lo + plane) % 2 * 4 + i
+        alone = 1 + half * 2 + dz if plane == 0 and dx == 0 else 0
         dest = (g, ((z_lo + dz) % 2 * 4 + x) * 2 + core)
         at = ((half * 2 + plane) * 2 + dz) * 4 + i
         slot = (half * 2 + (z_hi + dz) % 2) * 8 + y * 2 + dz
         remote = lambda: pltpu.make_async_remote_copy(
             src_ref=parts.at[at], dst_ref=sums.at[slot],
-            send_sem=part_send.at[at], recv_sem=part_recv,
+            send_sem=part_send.at[alone], recv_sem=part_recv,
             device_id=dest, device_id_type=MESH,
         )
         local = lambda: pltpu.make_async_copy(parts.at[at], sums.at[slot], part_recv)
         here = (dest[0] == grp) & (dest[1] == tp)
-        return at, remote, local, here
-
-    for slab in range(4):
-        own_copy(slab).wait()
-        old_copy(slab).wait_recv()
+        return remote, local, here
+
+    for which, sem in ((core, own_sem), (other, old_recv)):
+        rows = weight.at[:, pl.ds(pl.multiple_of(which * LOCAL, LOCAL), LOCAL)]
+        pltpu.make_async_copy(rows, rows, sem).wait()
     for half in range(2):
         rows = arrived.at[pl.ds(half * 256, 256)]
         pltpu.make_async_copy(rows, rows, delta_recv.at[half]).wait()
@@ -398,7 +397,10 @@
                         at = ((half * 2 + plane) * 2 + dz) * 4 + part
                         parts[at] = got[part * ALL:(part + 1) * ALL, dz * 128:dz * 128 + 128].astype(BF16)
                 for dx, dz in PART_ORDER:
-                    _, remote, local, here = part_copy(half, plane, dz, (x + dx) % 4)
+                    remote, local, here = part_copy(half, plane, dz, dx)
+                    if plane == 1 or dx > 0:
+                        remote().start()
+                        continue
 
                     @pl.when(here)
                     def _():
@@ -424,19 +426,18 @@
     def _():
         for half in range(2):
             delta_copy(7, half).wait_send()
-    for slab in range(4):
-        old_copy(slab).wait_send()
+    rows = weight.at[:, own_lanes]
+    pltpu.make_async_copy(rows, rows, old_send).wait()
     for k in range(6):
         square_copy(k).wait_send()
+    pltpu.make_async_copy(parts.at[pl.ds(0, 28)], parts.at[pl.ds(0, 28)], part_send.at[0]).wait()
     for half in range(2):
-        for plane in range(2):
-            for dz in range(2):
-                for i in range(4):
-                    _, remote, _, here = part_copy(half, plane, dz, i)
-
-                    @pl.when(jnp.logical_not(here))
-                    def _():
-                        remote().wait_send()
+        for dz in range(2):
+            remote, _, here = part_copy(half, 0, dz, 0)
+
+            @pl.when(jnp.logical_not(here))
+            def _():
+                remote().wait_send()
     pltpu.make_async_copy(sums, sums, part_recv).wait()
 
 
@@ -522,9 +523,9 @@
             pltpu.VMEM((32, ALL, 128), BF16),
             pltpu.VMEM((8, 128), F32),
             pltpu.VMEM((3, 8, 128), F32),
-            dma((10,)), dma((CHUNKS,)), dma((8,)), dma((4,)), dma((4,)), dma((4,)), dma((3,)), dma((2,)),
+            dma((10,)), dma((CHUNKS,)), dma((8,)), dma, dma, dma, dma((3,)), dma((2,)),
             dma, dma((7 * CHUNKS,)), dma, dma((2,)),
-            dma((32,)), dma, dma((6,)), dma((6,)),
+            dma((5,)), dma, dma((6,)), dma((6,)),
         ],
         compiler_params=pltpu.CompilerParams(
             collective_id=0, has_side_effects=True, vmem_limit_bytes=36 * 1024 * 1024

time: 38.5 us -> 37.1 us (0.964)
  Pallas kernels: 37.7 us -> 36.3 us
    pallas_call x1, Pallas kernels: 34.3 us -> 32.9 us  [local(): pl.pallas_call(mix_kernel, out_shape=(pltpu.VMEM(state_in.shape, F32), pl...]
where the time goes in v6:
time: 37.1 us; the launch traced here: 36.9 us
  Pallas kernels  36.3 us (98%)
  between operations  0.64 us (2%)
    pallas_call x1, Pallas kernels, local(): pl.pallas_call(mix_kernel, out_shape=(pltpu.VMEM(state_in.shape, F32), pl...  32.9 us
    pallas_call x1, Pallas kernels, local(): pl.pallas_call(finish_kernel, out_shape=(jax.ShapeDtypeStruct((STEPS, ROW...  3.37 us

profile of v6, /device:TPU:1, one launch (start us, length us, event | category | flops | bytes accessed | tf_op | source)
XLA Modules:
  0.0 36.9 jit_solution(13118021358881954014)
XLA Ops:
  0.6 32.9 %shard_map.140 = (f32[24,8,64,128]{3,2,1,0:T(8,128)S(1)}, bf16[32,96,128]{2,1,0:T(8,128)(2,1)S(1)}, f32[4,8,128]{2,1,0:T(8,128)S(1)}) custom-call(s32[64,8192]{1,0:T(8,128)} %codes_ref.1, s32[64,64]{1,0:T(8,128)} %exps_ref.1, bf16[8192,512]{1,0:T(8,128)(2,1)} %old_ref.1, f32[24,8,64,128]{3,2,1,0:T(8,128)} %state_ref.1, bf16[4,24,512]{2,1,0:T(8,128)(2,1)} %x_ref.1, ...), custom_call_target="tpu_custom_call" | custom-call | flops 900000000 | bytes 10000000 | tf_op jit(solution)/shard_map/pallas_call | solution.py:491
  33.6 3.4 %shard_map.141 = (bf16[4,24,512]{2,1,0:T(8,128)(2,1)}, f32[24,8,64,128]{3,2,1,0:T(8,128)}) custom-call(f32[24,8,64,128]{3,2,1,0:T(8,128)S(1)} %get-tuple-element.5.held, bf16[32,96,128]{2,1,0:T(8,128)(2,1)S(1)} %get-tuple-element.6.sums, f32[4,8,128]{2,1,0:T(8,128)S(1)} %get-tuple-element.7.squares), custom_call_target="tpu_custom_call" | custom-call | flops 1000000 | bytes 7000000 | tf_op jit(solution)/shard_map/pallas_call | solution.py:543

commit v7 on v6

--- a/solution.py
+++ b/solution.py
@@ -50,7 +50,7 @@
     )
 
 
-UNROLL = 4
+UNROLL = 8
 PART_ORDER = ((1, 0), (1, 1), (3, 0), (3, 1), (2, 0), (2, 1), (0, 0), (0, 1))
 OFFSETS = ((2, 0), (0, 1), (1, 0), (3, 1), (3, 0), (1, 1), (2, 1), (0, 0))
 GATHER = ((0, 1), (0, 3), (0, 2), (1, 0), (1, 1), (1, 3), (1, 2))

time: 37.1 us -> 36.9 us (level)
  no operation moved by 1% of the time
where the time goes in v7:
time: 36.9 us; the launch traced here: 36.6 us
  Pallas kernels  36 us (98%)
  between operations  0.64 us (2%)
    pallas_call x1, Pallas kernels, local(): pl.pallas_call(mix_kernel, out_shape=(pltpu.VMEM(state_in.shape, F32), pl...  32.6 us
    pallas_call x1, Pallas kernels, local(): pl.pallas_call(finish_kernel, out_shape=(jax.ShapeDtypeStruct((STEPS, ROW...  3.37 us

profile of v7, /device:TPU:1, one launch (start us, length us, event | category | flops | bytes accessed | tf_op | source)
XLA Modules:
  0.0 36.6 jit_solution(5188448289552172826)
XLA Ops:
  0.6 32.6 %shard_map.140 = (f32[24,8,64,128]{3,2,1,0:T(8,128)S(1)}, bf16[32,96,128]{2,1,0:T(8,128)(2,1)S(1)}, f32[4,8,128]{2,1,0:T(8,128)S(1)}) custom-call(s32[64,8192]{1,0:T(8,128)} %codes_ref.1, s32[64,64]{1,0:T(8,128)} %exps_ref.1, bf16[8192,512]{1,0:T(8,128)(2,1)} %old_ref.1, f32[24,8,64,128]{3,2,1,0:T(8,128)} %state_ref.1, bf16[4,24,512]{2,1,0:T(8,128)(2,1)} %x_ref.1, ...), custom_call_target="tpu_custom_call" | custom-call | flops 900000000 | bytes 10000000 | tf_op jit(solution)/shard_map/pallas_call | solution.py:491
  33.3 3.4 %shard_map.141 = (bf16[4,24,512]{2,1,0:T(8,128)(2,1)}, f32[24,8,64,128]{3,2,1,0:T(8,128)}) custom-call(f32[24,8,64,128]{3,2,1,0:T(8,128)S(1)} %get-tuple-element.5.held, bf16[32,96,128]{2,1,0:T(8,128)(2,1)S(1)} %get-tuple-element.6.sums, f32[4,8,128]{2,1,0:T(8,128)S(1)} %get-tuple-element.7.squares), custom_call_target="tpu_custom_call" | custom-call | flops 1000000 | bytes 7000000 | tf_op jit(solution)/shard_map/pallas_call | solution.py:543

commit v8 on v7

--- a/solution.py
+++ b/solution.py
@@ -155,7 +155,7 @@
         if k < 7:
             dl, dx = GATHER[k]
             slot = (z_lo + dl) % 2 * 4 + (x + 4 - dx) % 4
-        piece = acts.at[slot, pl.ds(c * SENT_ROWS, SENT_ROWS), own_lanes]
+        piece = acts.at[slot, pl.ds(0, ALL) if c is None else pl.ds(c * SENT_ROWS, SENT_ROWS), own_lanes]
         return pltpu.make_async_remote_copy(
             src_ref=piece, dst_ref=piece,
             send_sem=fwd_send, recv_sem=fwd_recv.at[0 if k in (7, 0, 1, 2) else 1],
@@ -273,6 +273,8 @@
     put(left_rows, 11 * ROWS, jnp.zeros((5 * ROWS, LOCAL), F32))
     square_rows[ALL:, :] = jnp.zeros((128 - ALL, 128), F32)
 
+    for slab in range(4):
+        own_copy(slab).start()
     pl.semaphore_wait(barrier, expected)
     for k in range(7):
         delta_copy(k, 0).start()
@@ -333,7 +335,6 @@
     for k in range(7):
         delta_copy(k, 1).start()
     for slab in range(4):
-        own_copy(slab).start()
         old_copy(slab).start()
 
     own_square[...] = jnp.transpose(square_rows[...])[0:8]
@@ -381,10 +382,10 @@
         for plane in range(2):
             if half == 0:
                 if plane == 1:
-                    for c in range(CHUNKS):
-                        for k in OTHER_PLANE:
+                    for k in OTHER_PLANE:
+                        for c in range(CHUNKS):
                             act_copy(c, k).wait_recv()
-                            fwd_copy(c, k).start()
+                        fwd_copy(None, k).start()
                 other_lanes = pl.ds(pl.multiple_of(other * LOCAL, LOCAL), LOCAL)
                 rows = acts.at[pl.ds((z_lo + plane) % 2 * 4, 4), :, other_lanes]
                 pltpu.make_async_copy(rows, rows, fwd_recv.at[plane]).wait()

time: 36.9 us -> 36.9 us (level)
  no operation moved by 1% of the time
where the time goes in v8:
time: 36.9 us; the launch traced here: 36.7 us
  Pallas kernels  36.1 us (98%)
  between operations  0.64 us (2%)
    pallas_call x1, Pallas kernels, local(): pl.pallas_call(mix_kernel, out_shape=(pltpu.VMEM(state_in.shape, F32), pl...  32.7 us
    pallas_call x1, Pallas kernels, local(): pl.pallas_call(finish_kernel, out_shape=(jax.ShapeDtypeStruct((STEPS, ROW...  3.37 us

profile of v8, /device:TPU:1, one launch (start us, length us, event | category | flops | bytes accessed | tf_op | source)
XLA Modules:
  0.0 36.7 jit_solution(14598063701508771399)
XLA Ops:
  0.6 32.7 %shard_map.140 = (f32[24,8,64,128]{3,2,1,0:T(8,128)S(1)}, bf16[32,96,128]{2,1,0:T(8,128)(2,1)S(1)}, f32[4,8,128]{2,1,0:T(8,128)S(1)}) custom-call(s32[64,8192]{1,0:T(8,128)} %codes_ref.1, s32[64,64]{1,0:T(8,128)} %exps_ref.1, bf16[8192,512]{1,0:T(8,128)(2,1)} %old_ref.1, f32[24,8,64,128]{3,2,1,0:T(8,128)} %state_ref.1, bf16[4,24,512]{2,1,0:T(8,128)(2,1)} %x_ref.1, ...), custom_call_target="tpu_custom_call" | custom-call | flops 900000000 | bytes 10000000 | tf_op jit(solution)/shard_map/pallas_call | solution.py:492
  33.4 3.4 %shard_map.141 = (bf16[4,24,512]{2,1,0:T(8,128)(2,1)}, f32[24,8,64,128]{3,2,1,0:T(8,128)}) custom-call(f32[24,8,64,128]{3,2,1,0:T(8,128)S(1)} %get-tuple-element.5.held, bf16[32,96,128]{2,1,0:T(8,128)(2,1)S(1)} %get-tuple-element.6.sums, f32[4,8,128]{2,1,0:T(8,128)S(1)} %get-tuple-element.7.squares), custom_call_target="tpu_custom_call" | custom-call | flops 1000000 | bytes 7000000 | tf_op jit(solution)/shard_map/pallas_call | solution.py:544

commit v9 on v8

--- a/solution.py
+++ b/solution.py
@@ -376,7 +376,7 @@
             first = q * 64 + half * 32
             coming = half * 256 + q * 32
             fresh.append(
-                (weight[first:first + 32, :].astype(F32) + arrived[coming:coming + 32, :].astype(F32)).astype(BF16)
+                weight[first:first + 32, :] + arrived[coming:coming + 32, :]
             )
         fresh = jnp.concatenate(fresh, axis=0)
         for plane in range(2):

time: 36.9 us -> 37 us (level)
  no operation moved by 1% of the time
where the time goes in v9:
time: 37 us; the launch traced here: 36.8 us
  Pallas kernels  36.1 us (98%)
  between operations  0.64 us (2%)
    pallas_call x1, Pallas kernels, local(): pl.pallas_call(mix_kernel, out_shape=(pltpu.VMEM(state_in.shape, F32), pl...  32.8 us
    pallas_call x1, Pallas kernels, local(): pl.pallas_call(finish_kernel, out_shape=(jax.ShapeDtypeStruct((STEPS, ROW...  3.37 us

profile of v9, /device:TPU:1, one launch (start us, length us, event | category | flops | bytes accessed | tf_op | source)
XLA Modules:
  0.0 36.8 jit_solution(2574976328092893276)
XLA Ops:
  0.6 32.8 %shard_map.140 = (f32[24,8,64,128]{3,2,1,0:T(8,128)S(1)}, bf16[32,96,128]{2,1,0:T(8,128)(2,1)S(1)}, f32[4,8,128]{2,1,0:T(8,128)S(1)}) custom-call(s32[64,8192]{1,0:T(8,128)} %codes_ref.1, s32[64,64]{1,0:T(8,128)} %exps_ref.1, bf16[8192,512]{1,0:T(8,128)(2,1)} %old_ref.1, f32[24,8,64,128]{3,2,1,0:T(8,128)} %state_ref.1, bf16[4,24,512]{2,1,0:T(8,128)(2,1)} %x_ref.1, ...), custom_call_target="tpu_custom_call" | custom-call | flops 900000000 | bytes 10000000 | tf_op jit(solution)/shard_map/pallas_call | solution.py:492
  33.4 3.4 %shard_map.141 = (bf16[4,24,512]{2,1,0:T(8,128)(2,1)}, f32[24,8,64,128]{3,2,1,0:T(8,128)}) custom-call(f32[24,8,64,128]{3,2,1,0:T(8,128)S(1)} %get-tuple-element.5.held, bf16[32,96,128]{2,1,0:T(8,128)(2,1)S(1)} %get-tuple-element.6.sums, f32[4,8,128]{2,1,0:T(8,128)S(1)} %get-tuple-element.7.squares), custom_call_target="tpu_custom_call" | custom-call | flops 1000000 | bytes 7000000 | tf_op jit(solution)/shard_map/pallas_call | solution.py:544
